TPU v7x, 512 devices: a whole 4x4x16 slice. The times are simulated.
512 devices in a mesh: panel: 128 (over y, z, core), obs: 4 (over x).
Axes of the slice: x: 4, y: 4, z: 16, core: 2. Of those that a mesh axis runs over, the one named last changes fastest.
Arguments:
- surface: float32 [4, 8, 2, 131072], P(None, None, None, 'panel'), may hold values from -6 to 6
- fluid_owner: int32 [32768, 1], P('panel'), may hold values from 0 to 127; in each aligned block of 256 rows (0 to 255, 256 to 511, ...) at most 8 rows name the same one
- cell_row: int32 [32768], P('panel'), may hold values from 0 to 1023
- pan_polar: float32 [32768], P('panel'), may hold values from 0 to 3.14159
- pan_azimuth: float32 [32768], P('panel'), may hold values from -3.140625 to 3.140625
- pan_radius: float32 [32768], P('panel'), may hold values from 0.8 to 1.2
- pan_area: float32 [32768], P('panel'), may hold values from 0.5 to 2
- obs_polar: float32 [16384], P(('panel', 'obs')), may hold values from 0 to 3.14159
- obs_azimuth: float32 [16384], P(('panel', 'obs')), may hold values from -3.140625 to 3.140625
- obs_distance: float32 [16384], P(('panel', 'obs')), may hold values from 5 to 20
- harmonic: int32 [2], replicated, may hold values from 1 to 8, as said below
Outputs:
- spectrum: float32 [2, 2, 16384], P(None, None, ('panel', 'obs'))
Inputs may be any that keep to these rules, and one draw needn't show every extreme that they name: `fluid_owner`: within the rows of one device (aligned blocks of 256 panels) no fluid owner is named by more than 8 panels, a bound that some block reaches. The 2 harmonic numbers differ, and one of them is 8.
All inputs are finite; a program needn't handle non-finite values.
Results may differ from a plain program's by a relative error of at most 0.0003.
Values sent between devices are 32-bit elements; how exact they have to be, the bound alone decides.
No kernel may reach another device: no remote copies, remote signals or barrier semaphores. Data moves between devices by JAX's collectives and lax.ppermute only.
A program may use at most 64 MiB of HBM per device.

v0:
```python
import math

import jax
import jax.numpy as jnp
from jax import lax
from jax.sharding import PartitionSpec as P

BASE_WAVE = 2.0


def directions(polar, azimuth):
    cycle = jnp.sin(polar)
    return jnp.stack([cycle * jnp.cos(azimuth), cycle * jnp.sin(azimuth), jnp.cos(polar)])


def sources(picked, normal, pan_area, panel_total):
    weight = pan_area * (1.0 / math.sqrt(panel_total))
    flux_real = (
        picked[1, :, 0] * normal[0] + picked[2, :, 0] * normal[1] + picked[3, :, 0] * normal[2]
    ) * weight
    flux_imag = (
        picked[1, :, 1] * normal[0] + picked[2, :, 1] * normal[1] + picked[3, :, 1] * normal[2]
    ) * weight
    press_real = picked[0, :, 0] * weight
    press_imag = picked[0, :, 1] * weight
    return (flux_real, flux_imag, press_real, press_imag)


def tile_sum(observer, panel_pos, normal, terms, waves):
    flux_real, flux_imag, press_real, press_imag = terms
    delta_x = observer[0][:, None] - panel_pos[0][None, :]
    delta_y = observer[1][:, None] - panel_pos[1][None, :]
    delta_z = observer[2][:, None] - panel_pos[2][None, :]
    distance = jnp.sqrt(delta_x * delta_x + delta_y * delta_y + delta_z * delta_z)
    inverse = 1.0 / distance
    cosine = (
        delta_x * normal[0][None, :] + delta_y * normal[1][None, :] + delta_z * normal[2][None, :]
    ) * inverse
    green_factor = inverse * (0.25 / math.pi)
    parts = []
    for which in range(waves.shape[0]):
        wave = waves[which]
        phase = wave * distance
        cos_phase = jnp.cos(phase)
        sin_phase = jnp.sin(phase)
        dip_real = press_real[which][None, :] * cosine
        dip_imag = press_imag[which][None, :] * cosine
        mix_real = -wave * flux_imag[which][None, :] + dip_real * inverse - wave * dip_imag
        mix_imag = wave * flux_real[which][None, :] + dip_imag * inverse + wave * dip_real
        parts.append(jnp.sum(green_factor * (cos_phase * mix_real + sin_phase * mix_imag), axis=1))
        parts.append(jnp.sum(green_factor * (cos_phase * mix_imag - sin_phase * mix_real), axis=1))
    return jnp.stack(parts).reshape(waves.shape[0], 2, observer.shape[1])


def local(
    surface,
    fluid_owner,
    cell_row,
    pan_polar,
    pan_azimuth,
    pan_radius,
    pan_area,
    obs_polar,
    obs_azimuth,
    obs_distance,
    harmonic,
):
    panel_count = lax.axis_size("panel")
    per_device = cell_row.shape[0]
    capacity = 4 * per_device // panel_count
    cell_count = surface.shape[3]
    owners = fluid_owner[:, 0]
    lanes = jnp.arange(panel_count, dtype=jnp.int32)
    member = (owners[:, None] == lanes[None, :]).astype(jnp.float32)
    positions = jnp.arange(per_device, dtype=jnp.int32)
    earlier = (positions[:, None] > positions[None, :]).astype(jnp.float32)
    before = jnp.dot(earlier, member, precision=lax.Precision.HIGHEST)
    rank_in_owner = jnp.sum(before * member, axis=1).astype(jnp.int32)
    slot_index = owners * capacity + rank_in_owner
    request = jnp.zeros((panel_count * capacity,), jnp.int32).at[slot_index].set(cell_row)
    wanted = lax.all_to_all(request, "panel", split_axis=0, concat_axis=0, tiled=True)
    choose = harmonic - 1
    pick_count = choose.shape[0]
    chosen = jnp.take(surface, choose, axis=1).reshape(-1, cell_count)
    outgoing = jnp.take(chosen, wanted, axis=1)
    arrived = lax.all_to_all(outgoing, "panel", split_axis=1, concat_axis=1, tiled=True)
    picked = jnp.take(arrived, slot_index, axis=1).reshape(
        surface.shape[0], pick_count, 2, per_device
    )
    normal = directions(pan_polar, pan_azimuth)
    panel_pos = normal * pan_radius[None, :]
    terms = sources(picked, normal, pan_area, per_device * panel_count)
    waves = BASE_WAVE * harmonic.astype(jnp.float32)
    all_polar, all_azimuth, all_distance = (
        lax.all_gather(obs_polar, "panel", axis=0, tiled=True),
        lax.all_gather(obs_azimuth, "panel", axis=0, tiled=True),
        lax.all_gather(obs_distance, "panel", axis=0, tiled=True),
    )
    observer = directions(all_polar, all_azimuth) * all_distance[None, :]
    local_count = observer.shape[1]
    block_size = 512
    blocks = observer.reshape(3, local_count // block_size, block_size).transpose(1, 0, 2)

    def one_block(piece):
        return tile_sum(piece, panel_pos, normal, terms, waves)

    partial_spectra = lax.map(one_block, blocks)
    partial_spectra = partial_spectra.transpose(1, 2, 0, 3).reshape(pick_count, 2, local_count)
    summed = lax.psum_scatter(partial_spectra, "panel", scatter_dimension=2, tiled=True)
    return summed * obs_distance[None, None, :]


def solution(mesh):
    in_specs = (
        P(None, None, None, "panel"),
        P("panel", None),
        P("panel"),
        P("panel"),
        P("panel"),
        P("panel"),
        P("panel"),
        P(("panel", "obs")),
        P(("panel", "obs")),
        P(("panel", "obs")),
        P(),
    )
    out_specs = P(None, None, ("panel", "obs"))
    return jax.shard_map(local, mesh=mesh, in_specs=in_specs, out_specs=out_specs, check_vma=False)
```

profile of v0, /device:TPU:1, one launch (start us, length us, event | category | flops | bytes accessed | tf_op | source)
XLA Modules:
  0.0 892.8 jit_solution(6697891631181781104)
XLA Ops:
  6.5 1.0 fusion.7
  8.2 1.6 scatter_custom_fusion
  10.5 20.6 %all-to-all-start = ((s32[128,8,1]{1,2,0:T(1,128)}), s32[128,8,1]{1,2,0:T(1,128)S(1)}, u32[]{:S(2)}, u32[]{:S(2)}) async-start(s32[128,8,1]{1,2,0:T(1,128)} %bitcast.35), calls=%async_computation | async-start | bytes 131072 | tf_op jit(solution)/shard_map/all_to_all | solution.py:81
  33.3 1.3 dynamic-slice
  35.3 0.9 dynamic-update-slice.1
  36.1 0.9 dynamic-update-slice
  37.0 0.9 dynamic-update-slice.2
  37.8 491.0 %all-reduce.3 = (f32[4096]{0:T(1024)S(1)}, f32[4096]{0:T(1024)S(1)}, f32[4096]{0:T(1024)S(1)}) all-reduce(f32[4096]{0:T(1024)S(1)} %dynamic-update-slice, f32[4096]{0:T(1024)S(1)} %dynamic-update-slice.1, f32[4096]{0:T(1024)S(1)} %dynamic-update-slice.2), channel_id=1, replica_groups=mesh['panel'=128,'obs'=4] {'panel'}, use_global_device_ids=true, to_apply=%add | all-reduce | flops 12288 | bytes 98304
  533.4 2.8 gather_fusion.1
  537.3 10.8 %all-to-all-start.1 = ((f32[128,1,128]{2,1,0:T(1,128)}), f32[128,1,128]{2,1,0:T(1,128)S(1)}, u32[]{:S(2)}, u32[]{:S(2)}) async-start(f32[128,1,128]{2,1,0:T(1,128)} %reshape.170), calls=%async_computation.1 | async-start | bytes 131072 | tf_op jit(solution)/shard_map/all_to_all | solution.py:86
  549.6 13.6 %all-to-all-done.1 = f32[128,1,128]{2,1,0:T(1,128)S(1)} async-done(((f32[128,1,128]{2,1,0:T(1,128)}), f32[128,1,128]{2,1,0:T(1,128)S(1)}, u32[]{:S(2)}, u32[]{:S(2)}) %all-to-all-start.1) | async-done | bytes 65568 | tf_op jit(solution)/shard_map/all_to_all | solution.py:86
  563.8 0.8 reduce.6
  565.8 67.8 %while.11 = (s32[]{:T(128)}, f32[8,2,2,512]{3,2,1,0:T(2,128)S(1)}, f32[8,3,512]{2,1,0:T(4,128)S(1)}, f32[3,256]{1,0:T(4,128)S(1)}, f32[2]{0:T(128)S(1)}, /*index...) while((s32[]{:T(128)}, f32[8,2,2,512]{3,2,1,0:T(2,128)S(1)}, ...), condition=%wide.region_7.8_spmd, body=%wide.region_2.7_spmd.sunk | while | flops 7607300 | bytes 112893 | solution.py:107
  566.5 1.3 slice_multiply_fusion.5
  567.8 6.4 multiply_reduce_fusion.5
  575.0 1.3 slice_multiply_fusion.5
  576.3 6.4 multiply_reduce_fusion.5
  583.4 1.3 slice_multiply_fusion.5
  584.7 6.4 multiply_reduce_fusion.5
  591.9 1.3 slice_multiply_fusion.5
  593.2 6.4 multiply_reduce_fusion.5
  600.4 1.3 slice_multiply_fusion.5
  601.7 6.4 multiply_reduce_fusion.5
  608.9 1.3 slice_multiply_fusion.5
  610.2 6.4 multiply_reduce_fusion.5
  617.4 1.3 slice_multiply_fusion.5
  618.7 6.4 multiply_reduce_fusion.5
  625.8 1.3 slice_multiply_fusion.5
  627.1 6.4 multiply_reduce_fusion.5
  633.6 4.4 copy.52
  638.1 5.4 reshape.156
  643.5 241.0 %reduce-scatter.4.cloned.1.call-done = f32[32,4]{1,0:T(8,128)} async-done(((f32[4096,4]{1,0:T(8,128)}), f32[32,4]{1,0:T(8,128)}) %reduce-scatter.4.cloned.1.call-update) | async-done | bytes 528
  (109 shorter events, 18.6 us)
Async XLA Ops:
  6.5 522.4 %copy-start = (f32[4,8,2,1024]{3,2,1,0:T(2,128)S(1)}, f32[4,8,2,1024]{3,2,1,0:T(2,128)}, u32[]{:S(2)}) copy-start(f32[4,8,2,1024]{3,2,1,0:T(2,128)} %param.13) | copy-start | bytes 786436
  10.5 521.4 %all-to-all-start = ((s32[128,8,1]{1,2,0:T(1,128)}), s32[128,8,1]{1,2,0:T(1,128)S(1)}, u32[]{:S(2)}, u32[]{:S(2)}) async-start(s32[128,8,1]{1,2,0:T(1,128)} %bitcast.35), calls=%async_computation | async-start | bytes 131072 | tf_op jit(solution)/shard_map/all_to_all | solution.py:81
  537.3 25.9 %all-to-all-start.1 = ((f32[128,1,128]{2,1,0:T(1,128)}), f32[128,1,128]{2,1,0:T(1,128)S(1)}, u32[]{:S(2)}, u32[]{:S(2)}) async-start(f32[128,1,128]{2,1,0:T(1,128)} %reshape.170), calls=%async_computation.1 | async-start | bytes 131072 | tf_op jit(solution)/shard_map/all_to_all | solution.py:86
  548.1 336.3 %reduce-scatter.4.cloned.1.call-start = ((), (), s32[]{:S(2)}) async-start(), calls=%async_computation.3 | async-start | bytes 2113536
  638.1 247.3 %copy-start.1 = (f32[32]{0:T(128)S(1)}, f32[32]{0:T(128)}, u32[]{:S(2)}) copy-start(f32[32]{0:T(128)} %param.22) | copy-start | bytes 388
Sparse Core Ops, SparseCore 0:
  643.6 240.7 reduce-scatter.3
where the time goes:
time: 904 us; the launch traced here: 893 us
  blocking collectives  491 us (54%)
  waiting for transfers between devices  255 us (28%)
  other arithmetic  67.8 us (8%)
  starting transfers between devices  31.6 us (3%)
  local copies, waits for them, and re-layouts  30.9 us (3%)
  between operations  15.5 us (2%)
    unnamed x1, blocking collectives  491 us
    unnamed x2, waiting for transfers between devices  241 us
    reduce_sum x8, other arithmetic, tile_sum(): jnp.sum(green_factor * (cos_phase * mix_real + sin_phase * mix_imag), axi...  51.5 us
    all_to_all x1, starting transfers between devices, local(): lax.all_to_all(request, 'panel', split_axis=0, concat_axis=0, tiled=True)  20.6 us
  transfers between devices with their start and end apart: 3, of which 2 were waited for; matrix products, arithmetic and copies ran while one was open for 1% of the time, Pallas kernels for 0%

commit v1 on v0

v1 whole, which is shorter than its diff:
```python
import functools
import math

import jax
import jax.numpy as jnp
from jax import lax
from jax.experimental import pallas as pl
from jax.experimental.pallas import tpu as pltpu
from jax.sharding import PartitionSpec as P

BASE_WAVE = 2.0
LANES = 128
SLOTS = 8
MAGIC = 12582912.0
F32 = jnp.float32
BF16 = jnp.bfloat16
VMEM_LIMIT = 48 * 1024 * 1024

SIN_HALF = (6.283164024353027, -10.334285736083984, 5.083797931671143, -1.1092723608016968)
COS_HALF = (1.9999998807907104, -9.869585990905762, 8.11682415008545, -2.6637604236602783, 0.4393935799598694)


def split3(value):
    high = value.astype(BF16).astype(F32)
    rest = value - high
    mid = rest.astype(BF16).astype(F32)
    return high, mid, rest - mid


def owner_mask(owner):
    rows = lax.broadcasted_iota(jnp.int32, (LANES, owner.shape[1]), 0)
    return jnp.where(rows == owner, 1.0, 0.0).astype(F32)


def rank_of(member):
    count = member.shape[1]
    first = lax.broadcasted_iota(jnp.int32, (count, count), 0)
    second = lax.broadcasted_iota(jnp.int32, (count, count), 1)
    earlier = jnp.where(first < second, 1.0, 0.0).astype(BF16)
    before = jnp.dot(member.astype(BF16), earlier, preferred_element_type=F32)
    return jnp.sum(before * member, axis=0, keepdims=True)


def ask_kernel(owner_ref, cell_ref, polar_ref, azimuth_ref, distance_ref, out_ref):
    member = owner_mask(owner_ref[...])
    rank = rank_of(member)
    cell = cell_ref[...]
    low = (cell & 31).astype(F32)
    high = (cell >> 5).astype(F32)
    slot = lax.broadcasted_iota(jnp.int32, (LANES, cell.shape[1]), 0)
    here = jnp.where((slot & 7).astype(F32) == rank, 1.0, 0.0)
    table = here * jnp.where(slot < 8, low, jnp.where(slot < 16, high, 0.0))
    asked = lax.dot_general(
        member.astype(BF16),
        table.astype(BF16),
        (((1,), (1,)), ((), ())),
        preferred_element_type=F32,
    )
    asked = asked + 32.0 * pltpu.roll(asked, LANES - 8, 1)
    lane = lax.broadcasted_iota(jnp.int32, (LANES, LANES), 1)
    polar = polar_ref[...]
    azimuth = azimuth_ref[...]
    distance = distance_ref[...]
    cycle = jnp.sin(polar) * distance
    place = jnp.concatenate(
        [
            jnp.zeros_like(polar),
            cycle * jnp.cos(azimuth),
            cycle * jnp.sin(azimuth),
            distance * jnp.cos(polar),
        ],
        axis=1,
    )
    out_ref[...] = jnp.where(lane < 8, asked, jnp.broadcast_to(place, (LANES, LANES)))


def pick_kernel(harmonic_ref, ask_ref, surface_ref, out_ref, rows_ref):
    wanted = jnp.transpose(ask_ref[...])[0:SLOTS].astype(jnp.int32)
    block = wanted >> 7
    within = wanted & 127
    chunks = surface_ref.shape[3] // LANES
    values = []
    for var in range(4):
        for which in range(2):
            values.append(surface_ref[var, harmonic_ref[which] - 1])
    values = jnp.concatenate(values, axis=0)
    for slot in range(SLOTS):
        index = jnp.broadcast_to(within[slot : slot + 1], (16, LANES))
        where = jnp.broadcast_to(block[slot : slot + 1], (16, LANES))
        found = jnp.zeros((16, LANES), F32)
        for chunk in range(chunks):
            part = values[:, chunk * LANES : (chunk + 1) * LANES]
            taken = jnp.take_along_axis(part, index, axis=1)
            found = jnp.where(where == chunk, taken, found)
        rows_ref[slot * 16 : slot * 16 + 16, :] = found
    out_ref[...] = jnp.transpose(rows_ref[...])


def radiate_kernel(
    harmonic_ref,
    ask_ref,
    answer_ref,
    owner_ref,
    polar_ref,
    azimuth_ref,
    radius_ref,
    area_ref,
    out_ref,
    panel_ref,
    observer_ref,
    linear_ref,
    rows_ref,
    *,
    panel_total,
):
    count = owner_ref.shape[1]
    member = owner_mask(owner_ref[...])
    rank = rank_of(member)
    spread = jnp.zeros((LANES, count), F32)
    for part in split3(answer_ref[...]):
        spread = spread + lax.dot_general(
            part.astype(BF16),
            member.astype(BF16),
            (((0,), (0,)), ((), ())),
            preferred_element_type=F32,
        )
    picked = jnp.zeros((16, count), F32)
    for slot in range(SLOTS):
        picked = picked + jnp.where(rank == slot, spread[slot * 16 : slot * 16 + 16], 0.0)

    polar = polar_ref[...]
    azimuth = azimuth_ref[...]
    radius = radius_ref[...]
    cycle = jnp.sin(polar)
    normal = (cycle * jnp.cos(azimuth), cycle * jnp.sin(azimuth), jnp.cos(polar))
    weight = area_ref[...] * (0.125 / (math.pi * math.sqrt(panel_total)))

    def row(var, which, part):
        at = var * 4 + which * 2 + part
        return picked[at : at + 1] * weight

    line = lax.broadcasted_iota(jnp.int32, (8, count), 0)

    def stack(*rows):
        total = jnp.zeros((8, count), F32)
        for at, value in enumerate(rows):
            total = jnp.where(line == at, value, total)
        return total

    square = stack(
        jnp.ones_like(radius),
        radius * radius,
        *[-2.0 * radius * axis for axis in normal],
    )
    offset = stack(jnp.zeros_like(radius), -radius, *normal)
    quantities = [square]
    for which in range(2):
        wave = BASE_WAVE * harmonic_ref[which].astype(F32)
        flux = [
            wave
            * (
                row(1, which, part) * normal[0]
                + row(2, which, part) * normal[1]
                + row(3, which, part) * normal[2]
            )
            for part in range(2)
        ]
        press = [row(0, which, part) for part in range(2)]
        quantities.append(square * (-flux[1]) + offset * press[0])
        quantities.append(square * flux[0] + offset * press[1])
        quantities.append(offset * (wave * press[0]))
        quantities.append(offset * (wave * press[1]))
    for number, quantity in enumerate(quantities):
        high, mid, low = split3(quantity)
        zero = jnp.zeros((80, count), F32)
        tall = jnp.concatenate([high, mid, low, high, mid, high, zero], axis=0)
        for half in range(count // LANES):
            panel_ref[pl.ds(number * count + half * LANES, LANES), :] = jnp.transpose(
                tall[:, half * LANES : (half + 1) * LANES]
            ).astype(BF16)

    place = jnp.transpose(ask_ref[...])
    few = lax.broadcasted_iota(jnp.int32, (8, LANES), 0)
    for number in range(32):
        axes = [place[32 * axis + number : 32 * axis + number + 1] for axis in (1, 2, 3)]
        dist = axes[0] * axes[0] + axes[1] * axes[1] + axes[2] * axes[2]
        total = jnp.where(few == 0, dist, jnp.where(few == 1, 1.0, 0.0))
        for at, value in enumerate(axes):
            total = jnp.where(few == at + 2, value, total)
        high, mid, low = split3(total)
        zero = jnp.zeros((80, LANES), F32)
        tall = jnp.concatenate([high, high, high, mid, mid, low, zero], axis=0)
        observer_ref[number // 2, :, (number % 2) * LANES : (number % 2 + 1) * LANES] = tall.astype(BF16)

    turns = [harmonic_ref[which].astype(F32) * (BASE_WAVE / (2.0 * math.pi)) for which in range(2)]

    def one_tile(tile, carry):
        linear_ref[...] = jnp.dot(panel_ref[...], observer_ref[tile], preferred_element_type=F32)
        for side in range(2):
            lanes = pl.ds(side * LANES, LANES)

            def group(step, sums):
                sums = list(sums)
                for sub in range(4):
                    base = pl.multiple_of(step * 32, 32) + sub * 8

                    def get(number):
                        return linear_ref[pl.ds(base + number * count, 8), lanes]

                    far = get(0)
                    inverse = lax.rsqrt(far)
                    distance = far * inverse
                    cube = inverse * inverse * inverse
                    for which in range(2):
                        phase = distance * turns[which]
                        phase = phase - ((phase + MAGIC) - MAGIC)
                        z = phase * phase
                        sine = SIN_HALF[-1]
                        for coef in SIN_HALF[-2::-1]:
                            sine = sine * z + coef
                        sine = sine * phase
                        cosine = COS_HALF[-1]
                        for coef in COS_HALF[-2::-1]:
                            cosine = cosine * z + coef
                        sine = sine * cosine
                        cosine = cosine * cosine - 2.0
                        sine = sine * cube
                        cosine = cosine * cube
                        real = get(1 + 4 * which) - distance * get(4 + 4 * which)
                        imag = get(2 + 4 * which) + distance * get(3 + 4 * which)
                        sums[2 * which] = sums[2 * which] + (cosine * real + sine * imag)
                        sums[2 * which + 1] = sums[2 * which + 1] + (cosine * imag - sine * real)
                return tuple(sums)

            zero = jnp.zeros((8, LANES), F32)
            sums = lax.fori_loop(0, count // 32, group, (zero,) * 4)
            for at in range(4):
                rows_ref[pl.ds(at * 32 + tile * 2 + side, 1), :] = jnp.sum(sums[at], axis=0, keepdims=True)
        return carry

    lax.fori_loop(0, 16, one_tile, 0)
    out_ref[...] = jnp.transpose(rows_ref[...])


def vmem():
    return pl.BlockSpec(memory_space=pltpu.VMEM)


def smem():
    return pl.BlockSpec(memory_space=pltpu.SMEM)


def exchange(value):
    return lax.all_to_all(value, "panel", split_axis=0, concat_axis=0, tiled=True)


def local(
    surface,
    fluid_owner,
    cell_row,
    pan_polar,
    pan_azimuth,
    pan_radius,
    pan_area,
    obs_polar,
    obs_azimuth,
    obs_distance,
    harmonic,
):
    per_device = cell_row.shape[0]
    panel_total = per_device * lax.axis_size("panel")
    owner = fluid_owner.reshape(1, per_device)
    table = jax.ShapeDtypeStruct((LANES, LANES), F32)
    params = pltpu.CompilerParams(vmem_limit_bytes=VMEM_LIMIT)
    ask = pl.pallas_call(
        ask_kernel,
        out_shape=table,
        in_specs=[vmem()] * 5,
        out_specs=vmem(),
        compiler_params=params,
        name="ask",
    )(
        owner,
        cell_row.reshape(1, per_device),
        obs_polar.reshape(1, -1),
        obs_azimuth.reshape(1, -1),
        obs_distance.reshape(1, -1),
    )
    ask = exchange(ask)
    answer = pl.pallas_call(
        pick_kernel,
        out_shape=table,
        in_specs=[smem(), vmem(), vmem()],
        out_specs=vmem(),
        scratch_shapes=[pltpu.VMEM((LANES, LANES), F32)],
        compiler_params=params,
        name="pick",
    )(harmonic, ask, surface)
    answer = exchange(answer)
    partial = pl.pallas_call(
        functools.partial(radiate_kernel, panel_total=panel_total),
        out_shape=table,
        in_specs=[smem()] + [vmem()] * 7,
        out_specs=vmem(),
        scratch_shapes=[
            pltpu.VMEM((9 * per_device, LANES), BF16),
            pltpu.VMEM((16, LANES, 2 * LANES), BF16),
            pltpu.VMEM((9 * per_device, 2 * LANES), F32),
            pltpu.VMEM((LANES, LANES), F32),
        ],
        compiler_params=params,
        name="radiate",
    )(
        harmonic,
        ask,
        answer,
        owner,
        pan_polar.reshape(1, -1),
        pan_azimuth.reshape(1, -1),
        pan_radius.reshape(1, -1),
        pan_area.reshape(1, -1),
    )
    partial = exchange(partial)
    summed = jnp.sum(partial, axis=0).reshape(2, 2, obs_distance.shape[0])
    return summed * obs_distance[None, None, :]


def solution(mesh):
    in_specs = (
        P(None, None, None, "panel"),
        P("panel", None),
        P("panel"),
        P("panel"),
        P("panel"),
        P("panel"),
        P("panel"),
        P(("panel", "obs")),
        P(("panel", "obs")),
        P(("panel", "obs")),
        P(),
    )
    out_specs = P(None, None, ("panel", "obs"))
    return jax.shard_map(local, mesh=mesh, in_specs=in_specs, out_specs=out_specs, check_vma=False)
```

time: 904 us -> 107 us (0.12); the launches traced: 893 us -> 106 us
  blocking collectives: 491 us -> 77.5 us
  waiting for transfers between devices: 255 us -> 0 us
  other arithmetic: 67.8 us -> 0.74 us
  starting transfers between devices: 31.6 us -> 0 us
  local copies, waits for them, and re-layouts: 30.9 us -> 3.12 us
  Pallas kernels: 0 us -> 24.9 us
  between operations: 15.5 us -> 0.05 us
    unnamed x1 -> x0, blocking collectives: 491 us -> none
    unnamed x2 -> x0, waiting for transfers between devices: 241 us -> none
    all_to_all x0 -> x3, blocking collectives: none -> 77.5 us  [exchange(): lax.all_to_all(value, 'panel', split_axis=0, concat_axis=0, tiled=True)]
    reduce_sum x8 -> x1, other arithmetic: 51.5 us -> 0.15 us  [local(): summed = jnp.sum(partial, axis=0).reshape(2, 2, obs_distance.shape[0])]
    all_to_all x2 -> x0, starting transfers between devices: 31.4 us -> none  [the longest x1 20.6 us: local(): lax.all_to_all(request, 'panel', split_axis=0, concat_axis=0, tiled=True)]
    pallas_call x0 -> x3, Pallas kernels: none -> 24.9 us  [the longest x1 23.5 us: local(): pl.pallas_call(functools.partial(radiate_kernel, panel_total=panel_total)...]
    all_to_all x2 -> x0, waiting for transfers between devices: 13.6 us -> none  [the longest x1 13.6 us: local(): lax.all_to_all(outgoing, 'panel', split_axis=1, concat_axis=1, tiled=True)]
    unnamed x17 -> x22, local copies, waits for them, and re-layouts: 15.6 us -> 3.03 us
  transfers between devices with their start and end apart: 3 -> 0, of which waited for: 2 -> 0; matrix products, arithmetic and copies ran while one was open for 1% -> 0% of each run, Pallas kernels for 0% -> 0%
where the time goes in v1:
time: 107 us; the launch traced here: 106 us
  blocking collectives  77.5 us (72%)
  Pallas kernels  24.9 us (23%)
  local copies, waits for them, and re-layouts  3.12 us (3%)
    all_to_all x3, blocking collectives, exchange(): lax.all_to_all(value, 'panel', split_axis=0, concat_axis=0, tiled=True)  77.5 us
    pallas_call x1, Pallas kernels, local(): pl.pallas_call(functools.partial(radiate_kernel, panel_total=panel_total)...  23.5 us
    unnamed x22, local copies, waits for them, and re-layouts  3.03 us

profile of v1, /device:TPU:1, one launch (start us, length us, event | category | flops | bytes accessed | tf_op | source)
XLA Modules:
  0.0 106.3 jit_solution(17381478951832314272)
XLA Ops:
  0.0 0.0 copy-start.4
  0.0 0.0 copy-start.9
  0.0 0.0 copy-start.10
  0.0 0.0 copy-start.1
  0.0 0.0 copy-start.3
  0.0 0.7 copy-done.4
  0.7 0.0 copy-done.9
  0.7 0.0 copy-done.10
  0.7 0.0 copy-done.1
  0.7 0.0 copy-done.3
  0.7 0.4 ask.1
  1.2 35.4 %all_to_all.31 = f32[128,1,128]{2,1,0:T(1,128)S(1)} all-to-all(f32[128,1,128]{2,1,0:T(1,128)S(1)} %bitcast.24), channel_id=1, replica_groups=mesh['panel'=128,'obs'=4] {'panel'}, dimensions={0} | all-to-all | bytes 131072 | tf_op jit(solution)/shard_map/all_to_all | solution.py:254
  36.6 0.0 copy-start.2
  36.6 0.7 copy-done.2
  37.3 0.0 copy-start
  37.3 0.9 copy-done
  38.2 0.9 pick.1
  39.1 21.1 %all_to_all.32 = f32[128,1,128]{2,1,0:T(1,128)S(1)} all-to-all(f32[128,1,128]{2,1,0:T(1,128)S(1)} %bitcast.25), channel_id=1, replica_groups=mesh['panel'=128,'obs'=4] {'panel'}, dimensions={0} | all-to-all | bytes 131072 | tf_op jit(solution)/shard_map/all_to_all | solution.py:254
  60.2 0.0 copy-start.6
  60.2 0.0 copy-start.7
  60.2 0.0 copy-start.8
  60.2 0.0 copy-start.5
  60.2 0.7 copy-done.6
  60.9 0.0 copy-done.7
  60.9 0.0 copy-done.8
  60.9 0.0 copy-done.5
  60.9 23.5 %radiate.1 = f32[128,128]{1,0:T(8,128)S(1)} custom-call(s32[2]{0:T(128)S(1)} %copy-done.2, f32[128,128]{1,0:T(8,128)S(1)} %bitcast.21, f32[128,128]{1,0:T(8,128)S(1)} %bitcast.22, s32[1,256]{1,0:T(1,128)S(1)} %bitcast.27, f32[1,256]{1,0:T(1,128)S(1)} %bitcast.30, f32[1,256]{1,0:T(1,128)S(1)} %bitcast.31, f32[1,256]{1,0:T(1,128)S(1)} %bitcast.32, ...), custom_call_target="tpu_custom_call" | custom-call | tf_op jit(solution)/shard_map/radiate/pallas_call | solution.py:300
  84.4 21.1 %all_to_all.33 = f32[128,1,128]{2,1,0:T(1,128)S(1)} all-to-all(f32[128,1,128]{2,1,0:T(1,128)S(1)} %bitcast.23), channel_id=1, replica_groups=mesh['panel'=128,'obs'=4] {'panel'}, dimensions={0} | all-to-all | bytes 131072 | tf_op jit(solution)/shard_map/all_to_all | solution.py:254
  105.5 0.2 reduce_sum.9
  105.7 0.1 reshape.46
  105.7 0.6 broadcast_multiply_fusion
Async XLA Ops:
  0.0 0.7 copy-start.4
  0.0 0.7 copy-start.9
  0.0 0.7 copy-start.10
  0.0 0.7 copy-start.1
  0.0 0.7 copy-start.3
  36.6 0.7 copy-start.2
  37.3 0.9 copy-start
  60.2 0.7 copy-start.6
  60.2 0.7 copy-start.7
  60.2 0.7 copy-start.8
  60.2 0.7 copy-start.5

commit v2 on v1

v2 whole, which is shorter than its diff:
```python
import functools
import math

import jax
import jax.numpy as jnp
from jax import lax
from jax.experimental import pallas as pl
from jax.experimental.pallas import tpu as pltpu
from jax.sharding import PartitionSpec as P

BASE_WAVE = 2.0
LANES = 128
SLOTS = 8
MAGIC = 12582912.0
F32 = jnp.float32
BF16 = jnp.bfloat16
VMEM_LIMIT = 48 * 1024 * 1024
TILES = 16

TAN_TOP = (3.1051745414733887, -2.988323211669922)
TAN_LOW = (0.9884211421012878, -4.203673839569092)


def split3(value):
    high = value.astype(BF16).astype(F32)
    rest = value - high
    mid = rest.astype(BF16).astype(F32)
    return high, mid, rest - mid


def owner_mask(owner):
    rows = lax.broadcasted_iota(jnp.int32, (LANES, owner.shape[1]), 0)
    return jnp.where(rows == owner, 1.0, 0.0).astype(F32)


def rank_of(member):
    count = member.shape[1]
    first = lax.broadcasted_iota(jnp.int32, (count, count), 0)
    second = lax.broadcasted_iota(jnp.int32, (count, count), 1)
    earlier = jnp.where(first < second, 1.0, 0.0).astype(BF16)
    before = jnp.dot(member.astype(BF16), earlier, preferred_element_type=F32)
    return jnp.sum(before * member, axis=0, keepdims=True)


def fetch(sources, targets, sem):
    copies = [pltpu.make_async_copy(*pair, sem.at[at]) for at, pair in enumerate(zip(sources, targets))]
    for copy in copies:
        copy.start()
    for copy in copies:
        copy.wait()


def ask_kernel(*refs):
    out_ref, owner_ref, cell_ref, polar_ref, azimuth_ref, distance_ref, sem = refs[5:]
    fetch(refs[:5], refs[6:11], sem)
    member = owner_mask(owner_ref[...])
    rank = rank_of(member)
    cell = cell_ref[...]
    low = (cell & 31).astype(F32)
    high = (cell >> 5).astype(F32)
    slot = lax.broadcasted_iota(jnp.int32, (LANES, cell.shape[1]), 0)
    here = jnp.where((slot & 7).astype(F32) == rank, 1.0, 0.0)
    table = here * jnp.where(slot < 8, low, jnp.where(slot < 16, high, 0.0))
    asked = lax.dot_general(
        member.astype(BF16),
        table.astype(BF16),
        (((1,), (1,)), ((), ())),
        preferred_element_type=F32,
    )
    asked = asked + 32.0 * pltpu.roll(asked, LANES - 8, 1)
    lane = lax.broadcasted_iota(jnp.int32, (LANES, LANES), 1)
    polar = polar_ref[...]
    azimuth = azimuth_ref[...]
    distance = distance_ref[...]
    cycle = jnp.sin(polar) * distance
    place = jnp.concatenate(
        [
            jnp.zeros_like(polar),
            cycle * jnp.cos(azimuth),
            cycle * jnp.sin(azimuth),
            distance * jnp.cos(polar),
        ],
        axis=1,
    )
    out_ref[...] = jnp.where(lane < 8, asked, jnp.broadcast_to(place, (LANES, LANES)))


def pick_kernel(ask_ref, values_ref, out_ref, rows_ref):
    wanted = jnp.transpose(ask_ref[...])[0:SLOTS].astype(jnp.int32)
    block = wanted >> 7
    within = wanted & 127
    values = values_ref[...]
    chunks = values.shape[1] // LANES
    for slot in range(SLOTS):
        index = jnp.broadcast_to(within[slot : slot + 1], (16, LANES))
        where = jnp.broadcast_to(block[slot : slot + 1], (16, LANES))
        found = jnp.zeros((16, LANES), F32)
        for chunk in range(chunks):
            part = values[:, chunk * LANES : (chunk + 1) * LANES]
            taken = jnp.take_along_axis(part, index, axis=1)
            found = jnp.where(where == chunk, taken, found)
        rows_ref[slot * 16 : slot * 16 + 16, :] = found
    out_ref[...] = jnp.transpose(rows_ref[...])


def prepare_kernel(harmonic_ref, after_ref, surface_ref, *refs, panel_total):
    values_ref, member_ref, info_ref, panel_ref = refs[5:9]
    rows_ref, owner_ref, polar_ref, azimuth_ref, radius_ref, area_ref, sem = refs[9:]
    sources = list(refs[:5])
    targets = [owner_ref, polar_ref, azimuth_ref, radius_ref, area_ref]
    for var in range(4):
        for which in range(2):
            sources.append(surface_ref.at[var, harmonic_ref[which] - 1])
            targets.append(rows_ref.at[2 * var + which])
    fetch(sources, targets, sem)
    for at in range(8):
        values_ref[2 * at : 2 * at + 2] = rows_ref[at]
    member = owner_mask(owner_ref[...])
    count = member.shape[1]
    member_ref[...] = member.astype(BF16)
    polar = polar_ref[...]
    azimuth = azimuth_ref[...]
    radius = radius_ref[...]
    cycle = jnp.sin(polar)
    normal = (cycle * jnp.cos(azimuth), cycle * jnp.sin(azimuth), jnp.cos(polar))
    line = lax.broadcasted_iota(jnp.int32, (8, count), 0)

    def stack(*rows):
        total = jnp.zeros((8, count), F32)
        for at, value in enumerate(rows):
            total = jnp.where(line == at, value, total)
        return total

    square = stack(
        jnp.ones_like(radius),
        radius * radius,
        *[-2.0 * radius * axis for axis in normal],
    )
    info_ref[0:8] = square
    info_ref[8:16] = stack(jnp.zeros_like(radius), -radius, *normal)
    weight = area_ref[...] * (0.25 / (math.pi * math.sqrt(panel_total)))
    waves = [BASE_WAVE * harmonic_ref[which].astype(F32) for which in range(2)]
    turns = [wave * (1.0 / (2.0 * math.pi)) for wave in waves]
    info_ref[16:24] = stack(rank_of(member), weight, *waves, *turns)

    zero = jnp.zeros((80, count), F32)
    for at, quantity in enumerate((square, info_ref[8:16])):
        high, mid, low = split3(quantity)
        tall = jnp.concatenate([high, mid, high, low, mid, high, zero], axis=0)
        for half in range(count // LANES):
            panel_ref[at, half * LANES : (half + 1) * LANES, :] = jnp.transpose(
                tall[:, half * LANES : (half + 1) * LANES]
            ).astype(BF16)


def observers_kernel(after_ref, ask_ref, observer_ref):
    place = jnp.transpose(ask_ref[...])
    few = lax.broadcasted_iota(jnp.int32, (8, LANES), 0)
    for number in range(32):
        axes = [place[32 * axis + number : 32 * axis + number + 1] for axis in (1, 2, 3)]
        dist = axes[0] * axes[0] + axes[1] * axes[1] + axes[2] * axes[2]
        total = jnp.where(few == 0, dist, jnp.where(few == 1, 1.0, 0.0))
        for at, value in enumerate(axes):
            total = jnp.where(few == at + 2, value, total)
        high, mid, low = split3(total)
        zero = jnp.zeros((80, LANES), F32)
        tall = jnp.concatenate([high, high, mid, high, mid, low, zero], axis=0)
        observer_ref[number // 2, :, (number % 2) * LANES : (number % 2 + 1) * LANES] = tall.astype(BF16)


def radiate_kernel(answer_ref, observer_ref, member_ref, info_ref, *refs):
    square_ref, out_ref, panel_ref, push_ref, even_ref, odd_ref, sums_ref = refs
    count = member_ref.shape[1]
    member = member_ref[...]
    spread = jnp.zeros((LANES, count), F32)
    for part in split3(answer_ref[...]):
        spread = spread + lax.dot_general(
            part.astype(BF16), member, (((0,), (0,)), ((), ())), preferred_element_type=F32
        )
    rank = info_ref[16:17]
    weight = info_ref[17:18]
    picked = jnp.zeros((16, count), F32)
    for slot in range(SLOTS):
        picked = picked + jnp.where(rank == slot, spread[slot * 16 : slot * 16 + 16], 0.0)
    picked = picked * weight
    square = info_ref[0:8]
    offset = info_ref[8:16]
    tall, push = [], []

    def place(number, start, lines):
        at = number * count + start
        panel_ref[at : at + lines.shape[0], :] = lines

    def row(var, which, part):
        at = var * 4 + which * 2 + part
        return picked[at : at + 1]

    for which in range(2):
        wave = info_ref[18 + which : 19 + which]
        flux = [
            wave
            * (
                row(1, which, part) * offset[2:3]
                + row(2, which, part) * offset[3:4]
                + row(3, which, part) * offset[4:5]
            )
            for part in range(2)
        ]
        press = [row(0, which, part) for part in range(2)]
        quantities = [offset * press[0] - square * flux[1], square * flux[0] + offset * press[1]]
        for quantity in quantities:
            high, mid, low = split3(quantity)
            tall += [high, mid, high, low]
        push += [wave * press[0], wave * press[1]]
    tall = jnp.concatenate(tall, axis=0)
    low_lanes = lax.broadcasted_iota(jnp.int32, (LANES, LANES), 1) < 32
    push = jnp.concatenate(push + [jnp.zeros((LANES - 4, count), F32)], axis=0)
    for half in range(count // LANES):
        here = slice(half * LANES, (half + 1) * LANES)
        turned = jnp.transpose(tall[:, here])
        for number in range(4):
            shifted = turned if number == 0 else pltpu.roll(turned, LANES - 32 * number, 1)
            place(number, half * LANES, jnp.where(low_lanes, shifted, 0.0).astype(BF16))
        turned = jnp.transpose(push[:, here])
        for number in range(4):
            push_ref[number, here, :] = jnp.broadcast_to(turned[:, number : number + 1], (LANES, LANES))
    for number in range(2):
        place(4 + number, 0, square_ref[number])

    turns = [jnp.broadcast_to(info_ref[20 + which : 21 + which, 0:LANES], (8, LANES)) for which in range(2)]

    def project(tile, linear_ref):
        linear_ref[...] = jnp.dot(panel_ref[...], observer_ref[tile], preferred_element_type=F32)

    def step(tile, now_ref, later_ref):
        project(jnp.minimum(tile + 1, TILES - 1), later_ref)
        sums = [jnp.zeros((8, LANES), F32)] * 8
        for first in range(0, count, 8):
            rows = slice(first, first + 8)
            push = [push_ref[number, rows, :] for number in range(4)]
            for side in range(2):
                lanes = slice(side * LANES, (side + 1) * LANES)

                def get(number):
                    return now_ref[number * count + first : number * count + first + 8, lanes]

                far = get(4)
                inverse = lax.rsqrt(far)
                distance = far * inverse
                shift = distance * get(5)
                cube = inverse * inverse * inverse
                twice = cube + cube
                for which in range(2):
                    phase = distance * turns[which]
                    phase = phase - ((phase + MAGIC) - MAGIC)
                    z = phase * phase
                    sine = phase * (TAN_TOP[0] + z * TAN_TOP[1])
                    cosine = (z + TAN_LOW[1]) * z + TAN_LOW[0]
                    scale = pl.reciprocal(sine * sine + cosine * cosine, approx=True)
                    part = sine * (scale * twice)
                    sine, cosine = cosine * part, cube - sine * part
                    real = get(2 * which) - shift * push[2 * which + 1]
                    imag = get(2 * which + 1) + shift * push[2 * which]
                    at = 2 * side + 4 * which
                    sums[at] = sums[at] + (cosine * real + sine * imag)
                    sums[at + 1] = sums[at + 1] + (cosine * imag - sine * real)
        for side in range(2):
            for at in range(4):
                line = at * 32 + tile * 2 + side
                value = sums[2 * side + 4 * (at // 2) + at % 2]
                sums_ref[pl.ds(pl.multiple_of(line * 8, 8), 8), :] = value

    project(0, even_ref)

    def one_tile(tile, carry):
        pl.when(tile % 2 == 0)(lambda: step(tile, even_ref, odd_ref))
        pl.when(tile % 2 == 1)(lambda: step(tile, odd_ref, even_ref))
        return carry

    lax.fori_loop(0, TILES, one_tile, 0)
    total = sums_ref[pl.ds(0, LANES, stride=8), :]
    for at in range(1, 8):
        total = total + sums_ref[pl.ds(at, LANES, stride=8), :]
    out_ref[...] = jnp.transpose(total)


def vmem():
    return pl.BlockSpec(memory_space=pltpu.VMEM)


def anywhere():
    return pl.BlockSpec(memory_space=pl.ANY)


def hbm():
    return pl.BlockSpec(memory_space=pltpu.HBM)


def smem():
    return pl.BlockSpec(memory_space=pltpu.SMEM)


def exchange(value):
    return lax.all_to_all(value, "panel", split_axis=0, concat_axis=0, tiled=True)


def local(
    surface,
    fluid_owner,
    cell_row,
    pan_polar,
    pan_azimuth,
    pan_radius,
    pan_area,
    obs_polar,
    obs_azimuth,
    obs_distance,
    harmonic,
):
    per_device = cell_row.shape[0]
    panel_total = per_device * lax.axis_size("panel")
    owner = fluid_owner.reshape(1, per_device)
    table = jax.ShapeDtypeStruct((LANES, LANES), F32)
    params = pltpu.CompilerParams(vmem_limit_bytes=VMEM_LIMIT)
    whole = pltpu.CompilerParams(vmem_limit_bytes=63 * 1024 * 1024)
    line = pltpu.VMEM((1, per_device), F32)
    few = pltpu.VMEM((1, obs_distance.shape[0]), F32)
    names = pltpu.VMEM((1, per_device), jnp.int32)
    ask = pl.pallas_call(
        ask_kernel,
        out_shape=table,
        in_specs=[hbm()] * 5,
        out_specs=vmem(),
        scratch_shapes=[names, names, few, few, few, pltpu.SemaphoreType.DMA((5,))],
        compiler_params=whole,
        name="ask",
    )(
        owner,
        cell_row.reshape(1, per_device),
        obs_polar.reshape(1, -1),
        obs_azimuth.reshape(1, -1),
        obs_distance.reshape(1, -1),
    )
    cells = surface.shape[3]
    values, member, info, square = pl.pallas_call(
        functools.partial(prepare_kernel, panel_total=panel_total),
        out_shape=(
            jax.ShapeDtypeStruct((16, cells), F32),
            jax.ShapeDtypeStruct((LANES, per_device), BF16),
            jax.ShapeDtypeStruct((24, per_device), F32),
            jax.ShapeDtypeStruct((2, per_device, LANES), BF16),
        ),
        in_specs=[smem(), anywhere()] + [hbm()] * 6,
        out_specs=(vmem(),) * 4,
        scratch_shapes=[
            pltpu.VMEM((8, 2, cells), F32),
            names,
            line,
            line,
            line,
            line,
            pltpu.SemaphoreType.DMA((13,)),
        ],
        compiler_params=params,
        cost_estimate=pl.CostEstimate(flops=10**7, bytes_accessed=10**7, transcendentals=0),
        name="prepare",
    )(
        harmonic,
        ask,
        surface,
        owner,
        pan_polar.reshape(1, -1),
        pan_azimuth.reshape(1, -1),
        pan_radius.reshape(1, -1),
        pan_area.reshape(1, -1),
    )
    asked = exchange(ask)
    found = pl.pallas_call(
        pick_kernel,
        out_shape=table,
        in_specs=[vmem()] * 2,
        out_specs=vmem(),
        scratch_shapes=[pltpu.VMEM((LANES, LANES), F32)],
        compiler_params=params,
        name="pick",
    )(asked, values)
    answer = exchange(found)
    pairs = per_device * 32 * LANES
    observer = pl.pallas_call(
        observers_kernel,
        out_shape=jax.ShapeDtypeStruct((TILES, LANES, 2 * LANES), BF16),
        in_specs=[anywhere(), vmem()],
        out_specs=vmem(),
        compiler_params=params,
        cost_estimate=pl.CostEstimate(flops=10**7, bytes_accessed=10**7, transcendentals=0),
        name="observers",
    )(found, asked)
    partial = pl.pallas_call(
        radiate_kernel,
        out_shape=table,
        in_specs=[vmem()] * 5,
        out_specs=vmem(),
        scratch_shapes=[
            pltpu.VMEM((6 * per_device, LANES), BF16),
            pltpu.VMEM((4, per_device, LANES), F32),
            pltpu.VMEM((6 * per_device, 2 * LANES), F32),
            pltpu.VMEM((6 * per_device, 2 * LANES), F32),
            pltpu.VMEM((8 * LANES, LANES), F32),
        ],
        compiler_params=params,
        cost_estimate=pl.CostEstimate(flops=90 * pairs, bytes_accessed=10**6, transcendentals=3 * pairs),
        name="radiate",
    )(answer, observer, member, info, square)
    partial = exchange(partial)
    summed = jnp.sum(partial, axis=0).reshape(2, 2, obs_distance.shape[0])
    return summed * obs_distance[None, None, :]


def solution(mesh):
    in_specs = (
        P(None, None, None, "panel"),
        P("panel", None),
        P("panel"),
        P("panel"),
        P("panel"),
        P("panel"),
        P("panel"),
        P(("panel", "obs")),
        P(("panel", "obs")),
        P(("panel", "obs")),
        P(),
    )
    out_specs = P(None, None, ("panel", "obs"))
    return jax.shard_map(local, mesh=mesh, in_specs=in_specs, out_specs=out_specs, check_vma=False)
```

time: 107 us -> 97.9 us (0.915)
  blocking collectives: 77.5 us -> 21.1 us
  starting transfers between devices: 0 us -> 27.3 us
  waiting for transfers between devices: 0 us -> 27.2 us
  Pallas kernels: 24.9 us -> 18.8 us
    all_to_all x3 -> x1, blocking collectives: 77.5 us -> 21.1 us  [exchange(): lax.all_to_all(value, 'panel', split_axis=0, concat_axis=0, tiled=True)]
    all_to_all x0 -> x2, starting transfers between devices: none -> 27.3 us  [exchange(): lax.all_to_all(value, 'panel', split_axis=0, concat_axis=0, tiled=True)]
    all_to_all x0 -> x2, waiting for transfers between devices: none -> 27.2 us  [exchange(): lax.all_to_all(value, 'panel', split_axis=0, concat_axis=0, tiled=True)]
    pallas_call x3 -> x5, Pallas kernels: 24.9 us -> 18.8 us  [the longest x1 14.8 us: local(): pl.pallas_call(radiate_kernel, out_shape=table, in_specs=[vmem()] * 5, ou...]
    unnamed x22 -> x18, local copies, waits for them, and re-layouts: 3.03 us -> 2.21 us
  transfers between devices with their start and end apart: 0 -> 2, of which waited for: 0 -> 2; matrix products, arithmetic and copies ran while one was open for 0% -> 0% of each run, Pallas kernels for 0% -> 1%
where the time goes in v2:
time: 97.9 us; the launch traced here: 97.6 us
  starting transfers between devices  27.3 us (28%)
  waiting for transfers between devices  27.2 us (28%)
  blocking collectives  21.1 us (22%)
  Pallas kernels  18.8 us (19%)
  local copies, waits for them, and re-layouts  2.3 us (2%)
    all_to_all x2, starting transfers between devices, exchange(): lax.all_to_all(value, 'panel', split_axis=0, concat_axis=0, tiled=True)  27.3 us
    all_to_all x2, waiting for transfers between devices, exchange(): lax.all_to_all(value, 'panel', split_axis=0, concat_axis=0, tiled=True)  27.2 us
    all_to_all x1, blocking collectives, exchange(): lax.all_to_all(value, 'panel', split_axis=0, concat_axis=0, tiled=True)  21.1 us
    pallas_call x1, Pallas kernels, local(): pl.pallas_call(radiate_kernel, out_shape=table, in_specs=[vmem()] * 5, ou...  14.8 us
    unnamed x18, local copies, waits for them, and re-layouts  2.21 us
  transfers between devices with their start and end apart: 2, of which 2 were waited for; matrix products, arithmetic and copies ran while one was open for 0% of the time, Pallas kernels for 1%

profile of v2, /device:TPU:1, one launch (start us, length us, event | category | flops | bytes accessed | tf_op | source)
XLA Modules:
  0.0 97.6 jit_solution(2407811721160302310)
XLA Ops:
  0.0 1.8 %ask.1.after_ref = f32[128,128]{1,0:T(8,128)} custom-call(s32[1,256]{1,0:T(1,128)} %bitcast.25, s32[1,256]{1,0:T(1,128)} %bitcast.32, f32[1,32]{1,0:T(1,128)} %bitcast.33, f32[1,32]{1,0:T(1,128)} %bitcast.34, f32[1,32]{1,0:T(1,128)} %bitcast.31), custom_call_target="tpu_custom_call" | custom-call | tf_op jit(solution)/shard_map/ask/pallas_call | solution.py:329
  1.8 0.0 copy-start
  1.8 20.7 %all-to-all-start = ((f32[128,1,128]{2,1,0:T(1,128)}), f32[128,1,128]{2,1,0:T(1,128)S(1)}, u32[]{:S(2)}, u32[]{:S(2)}) async-start(f32[128,1,128]{2,1,0:T(1,128)} %bitcast.22), calls=%async_computation | async-start | bytes 131072 | tf_op jit(solution)/shard_map/all_to_all | solution.py:304
  22.6 0.0 copy-start.3
  22.6 0.0 copy-start.4
  22.6 0.0 copy-start.5
  22.6 0.0 copy-start.6
  22.6 0.0 copy-start.2
  22.6 0.0 copy-start.7
  22.6 0.0 copy-done
  22.6 0.6 copy-done.3
  23.2 0.0 copy-done.4
  23.3 0.0 copy-done.5
  23.3 0.0 copy-done.6
  23.3 0.0 copy-done.2
  23.3 0.0 copy-done.7
  23.3 0.0 copy-start.1
  23.3 0.9 copy-done.1
  24.3 1.0 prepare.1
  25.2 12.3 %all-to-all-done = f32[128,1,128]{2,1,0:T(1,128)S(1)} async-done(((f32[128,1,128]{2,1,0:T(1,128)}), f32[128,1,128]{2,1,0:T(1,128)S(1)}, u32[]{:S(2)}, u32[]{:S(2)}) %all-to-all-start) | async-done | bytes 65568 | tf_op jit(solution)/shard_map/all_to_all | solution.py:304
  37.6 1.0 %pick.1.after_ref = f32[128,128]{1,0:T(8,128)} custom-call(f32[128,128]{1,0:T(8,128)S(1)} %bitcast.20, f32[16,1024]{1,0:T(8,128)S(1)} %get-tuple-element.9.values_ref), custom_call_target="tpu_custom_call" | custom-call | tf_op jit(solution)/shard_map/pick/pallas_call | solution.py:378
  38.6 6.6 %all-to-all-start.1 = ((f32[128,1,128]{2,1,0:T(1,128)}), f32[128,1,128]{2,1,0:T(1,128)S(1)}, u32[]{:S(2)}, u32[]{:S(2)}) async-start(f32[128,1,128]{2,1,0:T(1,128)} %bitcast.13), calls=%async_computation.1 | async-start | bytes 131072 | tf_op jit(solution)/shard_map/all_to_all | solution.py:304
  45.2 0.2 observers.1.observer_ref
  45.4 14.9 %all-to-all-done.1 = f32[128,1,128]{2,1,0:T(1,128)S(1)} async-done(((f32[128,1,128]{2,1,0:T(1,128)}), f32[128,1,128]{2,1,0:T(1,128)S(1)}, u32[]{:S(2)}, u32[]{:S(2)}) %all-to-all-start.1) | async-done | bytes 65568 | tf_op jit(solution)/shard_map/all_to_all | solution.py:304
  60.3 14.8 %radiate.1 = f32[128,128]{1,0:T(8,128)S(1)} custom-call(f32[128,128]{1,0:T(8,128)S(1)} %bitcast.23, bf16[16,128,256]{2,1,0:T(8,128)(2,1)S(1)} %observers.1.observer_ref, bf16[128,256]{1,0:T(8,128)(2,1)S(1)} %get-tuple-element.10.member_ref, f32[24,256]{1,0:T(8,128)S(1)} %get-tuple-element.11.info_ref, bf16[2,256,128]{2,1,0:T(8,128)(2,1)S(1)} %get-tuple-element.12.refs_0_), custom_call_target="tpu_custom_call" | custom-call | flops 94371840 | bytes 1000000 | tf_op jit(solution)/shard_map/radiate/pallas_call | solution.py:398
  75.1 21.1 %all_to_all.31 = f32[128,1,128]{2,1,0:T(1,128)S(1)} all-to-all(f32[128,1,128]{2,1,0:T(1,128)S(1)} %bitcast.24), channel_id=1, replica_groups=mesh['panel'=128,'obs'=4] {'panel'}, dimensions={0} | all-to-all | bytes 131072 | tf_op jit(solution)/shard_map/all_to_all | solution.py:304
  96.2 0.2 reduce_sum.9
  96.4 0.0 copy-start.8
  96.4 0.1 reshape.46
  96.4 0.6 copy-done.8
  97.0 0.6 broadcast_multiply_fusion
Async XLA Ops:
  1.8 20.8 %copy-start = (f32[128,128]{1,0:T(8,128)S(1)}, f32[128,128]{1,0:T(8,128)}, u32[]{:S(2)}) copy-start(f32[128,128]{1,0:T(8,128)} %ask.1.after_ref) | copy-start | bytes 196612
  1.8 35.7 %all-to-all-start = ((f32[128,1,128]{2,1,0:T(1,128)}), f32[128,1,128]{2,1,0:T(1,128)S(1)}, u32[]{:S(2)}, u32[]{:S(2)}) async-start(f32[128,1,128]{2,1,0:T(1,128)} %bitcast.22), calls=%async_computation | async-start | bytes 131072 | tf_op jit(solution)/shard_map/all_to_all | solution.py:304
  22.6 0.7 copy-start.3
  22.6 0.7 copy-start.4
  22.6 0.7 copy-start.5
  22.6 0.7 copy-start.6
  22.6 0.7 copy-start.2
  22.6 0.7 copy-start.7
  23.3 1.0 copy-start.1
  38.6 21.7 %all-to-all-start.1 = ((f32[128,1,128]{2,1,0:T(1,128)}), f32[128,1,128]{2,1,0:T(1,128)S(1)}, u32[]{:S(2)}, u32[]{:S(2)}) async-start(f32[128,1,128]{2,1,0:T(1,128)} %bitcast.13), calls=%async_computation.1 | async-start | bytes 131072 | tf_op jit(solution)/shard_map/all_to_all | solution.py:304
  96.4 0.7 copy-start.8

commit v3 on v2

--- a/solution.py
+++ b/solution.py
@@ -10,12 +10,14 @@
 
 BASE_WAVE = 2.0
 LANES = 128
-SLOTS = 8
+CHIPS = 64
+SLOTS = 16
 MAGIC = 12582912.0
 F32 = jnp.float32
 BF16 = jnp.bfloat16
 VMEM_LIMIT = 48 * 1024 * 1024
 TILES = 16
+JOIN = 1
 
 TAN_TOP = (3.1051745414733887, -2.988323211669922)
 TAN_LOW = (0.9884211421012878, -4.203673839569092)
@@ -42,6 +44,15 @@
     return jnp.sum(before * member, axis=0, keepdims=True)
 
 
+def chip_mask(owner):
+    rows = lax.broadcasted_iota(jnp.int32, (CHIPS, owner.shape[1]), 0)
+    return jnp.where(rows == (owner >> 1), 1.0, 0.0).astype(F32)
+
+
+def slot_of(owner):
+    return rank_of(owner_mask(owner)) + (8 * (owner & 1)).astype(F32)
+
+
 def fetch(sources, targets, sem):
     copies = [pltpu.make_async_copy(*pair, sem.at[at]) for at, pair in enumerate(zip(sources, targets))]
     for copy in copies:
@@ -53,22 +64,22 @@
 def ask_kernel(*refs):
     out_ref, owner_ref, cell_ref, polar_ref, azimuth_ref, distance_ref, sem = refs[5:]
     fetch(refs[:5], refs[6:11], sem)
-    member = owner_mask(owner_ref[...])
-    rank = rank_of(member)
+    owner = owner_ref[...]
+    place = slot_of(owner)
     cell = cell_ref[...]
     low = (cell & 31).astype(F32)
     high = (cell >> 5).astype(F32)
     slot = lax.broadcasted_iota(jnp.int32, (LANES, cell.shape[1]), 0)
-    here = jnp.where((slot & 7).astype(F32) == rank, 1.0, 0.0)
-    table = here * jnp.where(slot < 8, low, jnp.where(slot < 16, high, 0.0))
+    here = jnp.where((slot & 15).astype(F32) == place, 1.0, 0.0)
+    table = here * jnp.where(slot < 16, low, jnp.where(slot < 32, high, 0.0))
     asked = lax.dot_general(
-        member.astype(BF16),
+        chip_mask(owner).astype(BF16),
         table.astype(BF16),
         (((1,), (1,)), ((), ())),
         preferred_element_type=F32,
     )
-    asked = asked + 32.0 * pltpu.roll(asked, LANES - 8, 1)
-    lane = lax.broadcasted_iota(jnp.int32, (LANES, LANES), 1)
+    asked = asked + 32.0 * pltpu.roll(asked, LANES - 16, 1)
+    lane = lax.broadcasted_iota(jnp.int32, (CHIPS, LANES), 1)
     polar = polar_ref[...]
     azimuth = azimuth_ref[...]
     distance = distance_ref[...]
@@ -82,25 +93,30 @@
         ],
         axis=1,
     )
-    out_ref[...] = jnp.where(lane < 8, asked, jnp.broadcast_to(place, (LANES, LANES)))
-
-
-def pick_kernel(ask_ref, values_ref, out_ref, rows_ref):
-    wanted = jnp.transpose(ask_ref[...])[0:SLOTS].astype(jnp.int32)
+    out_ref[...] = jnp.where(lane < 16, asked, jnp.broadcast_to(place, (CHIPS, LANES)))
+
+
+def pick_kernel(ask_ref, own_ref, mate_ref, out_ref, rows_ref):
+    square = jnp.concatenate([ask_ref[...], jnp.zeros((LANES - CHIPS, LANES), F32)], axis=0)
+    wanted = jnp.transpose(square)[0:SLOTS].astype(jnp.int32)
     block = wanted >> 7
     within = wanted & 127
-    values = values_ref[...]
-    chunks = values.shape[1] // LANES
+    first = lax.axis_index("panel") % 2 == 0
+    own, mate = own_ref[...], mate_ref[...]
+    values = (jnp.where(first, own, mate), jnp.where(first, mate, own))
+    chunks = own.shape[1] // LANES
     for slot in range(SLOTS):
         index = jnp.broadcast_to(within[slot : slot + 1], (16, LANES))
         where = jnp.broadcast_to(block[slot : slot + 1], (16, LANES))
         found = jnp.zeros((16, LANES), F32)
         for chunk in range(chunks):
-            part = values[:, chunk * LANES : (chunk + 1) * LANES]
+            part = values[slot // 8][:, chunk * LANES : (chunk + 1) * LANES]
             taken = jnp.take_along_axis(part, index, axis=1)
             found = jnp.where(where == chunk, taken, found)
         rows_ref[slot * 16 : slot * 16 + 16, :] = found
-    out_ref[...] = jnp.transpose(rows_ref[...])
+    for half in range(2):
+        here = slice(half * LANES, (half + 1) * LANES)
+        out_ref[pl.ds(half, CHIPS, stride=2), :] = jnp.transpose(rows_ref[here, :])[0:CHIPS]
 
 
 def prepare_kernel(harmonic_ref, after_ref, surface_ref, *refs, panel_total):
@@ -115,9 +131,9 @@
     fetch(sources, targets, sem)
     for at in range(8):
         values_ref[2 * at : 2 * at + 2] = rows_ref[at]
-    member = owner_mask(owner_ref[...])
-    count = member.shape[1]
-    member_ref[...] = member.astype(BF16)
+    owner = owner_ref[...]
+    count = owner.shape[1]
+    member_ref[...] = chip_mask(owner).astype(BF16)
     polar = polar_ref[...]
     azimuth = azimuth_ref[...]
     radius = radius_ref[...]
@@ -141,7 +157,7 @@
     weight = area_ref[...] * (0.25 / (math.pi * math.sqrt(panel_total)))
     waves = [BASE_WAVE * harmonic_ref[which].astype(F32) for which in range(2)]
     turns = [wave * (1.0 / (2.0 * math.pi)) for wave in waves]
-    info_ref[16:24] = stack(rank_of(member), weight, *waves, *turns)
+    info_ref[16:24] = stack(slot_of(owner), weight, *waves, *turns)
 
     zero = jnp.zeros((80, count), F32)
     for at, quantity in enumerate((square, info_ref[8:16])):
@@ -153,13 +169,18 @@
             ).astype(BF16)
 
 
-def observers_kernel(after_ref, ask_ref, observer_ref):
-    place = jnp.transpose(ask_ref[...])
+def observers_kernel(own_ref, mate_ref, observer_ref, distance_ref, rows_ref):
+    first = lax.axis_index("panel") % 2 == 0
+    own, mate = own_ref[...], mate_ref[...]
+    rows_ref[pl.ds(0, CHIPS, stride=2), :] = jnp.where(first, own, mate)
+    rows_ref[pl.ds(1, CHIPS, stride=2), :] = jnp.where(first, mate, own)
+    place = jnp.transpose(rows_ref[...])
+    far = place[32:64] * place[32:64] + place[64:96] * place[64:96] + place[96:128] * place[96:128]
+    distance_ref[...] = jnp.sqrt(far)
     few = lax.broadcasted_iota(jnp.int32, (8, LANES), 0)
     for number in range(32):
         axes = [place[32 * axis + number : 32 * axis + number + 1] for axis in (1, 2, 3)]
-        dist = axes[0] * axes[0] + axes[1] * axes[1] + axes[2] * axes[2]
-        total = jnp.where(few == 0, dist, jnp.where(few == 1, 1.0, 0.0))
+        total = jnp.where(few == 0, far[number : number + 1], jnp.where(few == 1, 1.0, 0.0))
         for at, value in enumerate(axes):
             total = jnp.where(few == at + 2, value, total)
         high, mid, low = split3(total)
@@ -168,20 +189,22 @@
         observer_ref[number // 2, :, (number % 2) * LANES : (number % 2 + 1) * LANES] = tall.astype(BF16)
 
 
-def radiate_kernel(answer_ref, observer_ref, member_ref, info_ref, *refs):
+def radiate_kernel(answer_ref, observer_ref, distance_ref, member_ref, info_ref, *refs):
     square_ref, out_ref, panel_ref, push_ref, even_ref, odd_ref, sums_ref = refs
     count = member_ref.shape[1]
     member = member_ref[...]
-    spread = jnp.zeros((LANES, count), F32)
-    for part in split3(answer_ref[...]):
-        spread = spread + lax.dot_general(
-            part.astype(BF16), member, (((0,), (0,)), ((), ())), preferred_element_type=F32
-        )
+    spread = [jnp.zeros((LANES, count), F32)] * 2
+    for half in range(2):
+        for part in split3(answer_ref[pl.ds(half, CHIPS, stride=2), :]):
+            spread[half] = spread[half] + lax.dot_general(
+                part.astype(BF16), member, (((0,), (0,)), ((), ())), preferred_element_type=F32
+            )
     rank = info_ref[16:17]
     weight = info_ref[17:18]
     picked = jnp.zeros((16, count), F32)
     for slot in range(SLOTS):
-        picked = picked + jnp.where(rank == slot, spread[slot * 16 : slot * 16 + 16], 0.0)
+        lines = spread[slot // 8][slot % 8 * 16 : slot % 8 * 16 + 16]
+        picked = picked + jnp.where(rank == slot, lines, 0.0)
     picked = picked * weight
     square = info_ref[0:8]
     offset = info_ref[8:16]
@@ -229,17 +252,21 @@
 
     turns = [jnp.broadcast_to(info_ref[20 + which : 21 + which, 0:LANES], (8, LANES)) for which in range(2)]
 
-    def project(tile, linear_ref):
-        linear_ref[...] = jnp.dot(panel_ref[...], observer_ref[tile], preferred_element_type=F32)
-
-    def step(tile, now_ref, later_ref):
-        project(jnp.minimum(tile + 1, TILES - 1), later_ref)
-        sums = [jnp.zeros((8, LANES), F32)] * 8
-        for first in range(0, count, 8):
-            rows = slice(first, first + 8)
-            push = [push_ref[number, rows, :] for number in range(4)]
-            for side in range(2):
-                lanes = slice(side * LANES, (side + 1) * LANES)
+    def project(step, linear_ref):
+        views = jnp.concatenate([observer_ref[step * JOIN + at] for at in range(JOIN)], axis=1)
+        linear_ref[...] = jnp.dot(panel_ref[...], views, preferred_element_type=F32)
+
+    def tiles(step, now_ref, later_ref):
+        for side in range(2 * JOIN):
+            lanes = slice(side * LANES, (side + 1) * LANES)
+            sums = [jnp.zeros((8, LANES), F32)] * 4
+            for first in range(0, count, 8):
+                if first % 64 == 0 and side * 4 + first // 64 < 6:
+                    number = side * 4 + first // 64
+                    lines = pl.ds(number * count, count)
+                    following = observer_ref[jnp.minimum(step + 1, TILES // JOIN - 1)]
+                    later_ref[lines, :] = jnp.dot(panel_ref[lines, :], following, preferred_element_type=F32)
+                rows = slice(first, first + 8)
 
                 def get(number):
                     return now_ref[number * count + first : number * count + first + 8, lanes]
@@ -252,35 +279,33 @@
                 twice = cube + cube
                 for which in range(2):
                     phase = distance * turns[which]
-                    phase = phase - ((phase + MAGIC) - MAGIC)
+                    phase = phase - jnp.round(phase)
                     z = phase * phase
                     sine = phase * (TAN_TOP[0] + z * TAN_TOP[1])
                     cosine = (z + TAN_LOW[1]) * z + TAN_LOW[0]
                     scale = pl.reciprocal(sine * sine + cosine * cosine, approx=True)
                     part = sine * (scale * twice)
                     sine, cosine = cosine * part, cube - sine * part
-                    real = get(2 * which) - shift * push[2 * which + 1]
-                    imag = get(2 * which + 1) + shift * push[2 * which]
-                    at = 2 * side + 4 * which
-                    sums[at] = sums[at] + (cosine * real + sine * imag)
-                    sums[at + 1] = sums[at + 1] + (cosine * imag - sine * real)
-        for side in range(2):
+                    real = get(2 * which) - shift * push_ref[2 * which + 1, rows, :]
+                    imag = get(2 * which + 1) + shift * push_ref[2 * which, rows, :]
+                    sums[2 * which] = sums[2 * which] + (cosine * real + sine * imag)
+                    sums[2 * which + 1] = sums[2 * which + 1] + (cosine * imag - sine * real)
             for at in range(4):
-                line = at * 32 + tile * 2 + side
-                value = sums[2 * side + 4 * (at // 2) + at % 2]
-                sums_ref[pl.ds(pl.multiple_of(line * 8, 8), 8), :] = value
+                line = at * 32 + step * 2 * JOIN + side
+                sums_ref[pl.ds(pl.multiple_of(line * 8, 8), 8), :] = sums[at]
 
     project(0, even_ref)
 
-    def one_tile(tile, carry):
-        pl.when(tile % 2 == 0)(lambda: step(tile, even_ref, odd_ref))
-        pl.when(tile % 2 == 1)(lambda: step(tile, odd_ref, even_ref))
+    def one_step(step, carry):
+        pl.when(step % 2 == 0)(lambda: tiles(step, even_ref, odd_ref))
+        pl.when(step % 2 == 1)(lambda: tiles(step, odd_ref, even_ref))
         return carry
 
-    lax.fori_loop(0, TILES, one_tile, 0)
+    lax.fori_loop(0, TILES // JOIN, one_step, 0)
     total = sums_ref[pl.ds(0, LANES, stride=8), :]
     for at in range(1, 8):
         total = total + sums_ref[pl.ds(at, LANES, stride=8), :]
+    total = total * jnp.concatenate([distance_ref[...]] * 4, axis=0)
     out_ref[...] = jnp.transpose(total)
 
 
@@ -300,8 +325,17 @@
     return pl.BlockSpec(memory_space=pltpu.SMEM)
 
 
-def exchange(value):
-    return lax.all_to_all(value, "panel", split_axis=0, concat_axis=0, tiled=True)
+SAME_CORE = [[2 * chip + core for chip in range(CHIPS)] for core in range(2)]
+
+
+def exchange(value, groups=None):
+    return lax.all_to_all(
+        value, "panel", split_axis=0, concat_axis=0, axis_index_groups=groups, tiled=True
+    )
+
+
+def swap(value):
+    return lax.ppermute(value, "panel", [(at, at ^ 1) for at in range(2 * CHIPS)])
 
 
 def local(
@@ -328,7 +362,7 @@
     names = pltpu.VMEM((1, per_device), jnp.int32)
     ask = pl.pallas_call(
         ask_kernel,
-        out_shape=table,
+        out_shape=jax.ShapeDtypeStruct((CHIPS, LANES), F32),
         in_specs=[hbm()] * 5,
         out_specs=vmem(),
         scratch_shapes=[names, names, few, few, few, pltpu.SemaphoreType.DMA((5,))],
@@ -346,7 +380,7 @@
         functools.partial(prepare_kernel, panel_total=panel_total),
         out_shape=(
             jax.ShapeDtypeStruct((16, cells), F32),
-            jax.ShapeDtypeStruct((LANES, per_device), BF16),
+            jax.ShapeDtypeStruct((CHIPS, per_device), BF16),
             jax.ShapeDtypeStruct((24, per_device), F32),
             jax.ShapeDtypeStruct((2, per_device, LANES), BF16),
         ),
@@ -374,46 +408,52 @@
         pan_radius.reshape(1, -1),
         pan_area.reshape(1, -1),
     )
-    asked = exchange(ask)
+    mate_values = swap(values)
+    asked = exchange(ask, SAME_CORE)
     found = pl.pallas_call(
         pick_kernel,
         out_shape=table,
-        in_specs=[vmem()] * 2,
+        in_specs=[vmem()] * 3,
         out_specs=vmem(),
-        scratch_shapes=[pltpu.VMEM((LANES, LANES), F32)],
+        scratch_shapes=[pltpu.VMEM((SLOTS * 16, LANES), F32)],
         compiler_params=params,
         name="pick",
-    )(asked, values)
-    answer = exchange(found)
+    )(asked, values, mate_values)
+    answer = exchange(found, SAME_CORE)
+    asked, _ = lax.optimization_barrier((asked, found))
+    mate_asked = swap(asked)
     pairs = per_device * 32 * LANES
-    observer = pl.pallas_call(
+    observer, distance = pl.pallas_call(
         observers_kernel,
-        out_shape=jax.ShapeDtypeStruct((TILES, LANES, 2 * LANES), BF16),
-        in_specs=[anywhere(), vmem()],
-        out_specs=vmem(),
+        out_shape=(
+            jax.ShapeDtypeStruct((TILES, LANES, 2 * LANES), BF16),
+            jax.ShapeDtypeStruct((32, LANES), F32),
+        ),
+        in_specs=[vmem()] * 2,
+        out_specs=(vmem(),) * 2,
+        scratch_shapes=[pltpu.VMEM((LANES, LANES), F32)],
         compiler_params=params,
         cost_estimate=pl.CostEstimate(flops=10**7, bytes_accessed=10**7, transcendentals=0),
         name="observers",
-    )(found, asked)
+    )(asked, mate_asked)
     partial = pl.pallas_call(
         radiate_kernel,
         out_shape=table,
-        in_specs=[vmem()] * 5,
+        in_specs=[vmem()] * 6,
         out_specs=vmem(),
         scratch_shapes=[
             pltpu.VMEM((6 * per_device, LANES), BF16),
             pltpu.VMEM((4, per_device, LANES), F32),
-            pltpu.VMEM((6 * per_device, 2 * LANES), F32),
-            pltpu.VMEM((6 * per_device, 2 * LANES), F32),
+            pltpu.VMEM((6 * per_device, 2 * JOIN * LANES), F32),
+            pltpu.VMEM((6 * per_device, 2 * JOIN * LANES), F32),
             pltpu.VMEM((8 * LANES, LANES), F32),
         ],
         compiler_params=params,
         cost_estimate=pl.CostEstimate(flops=90 * pairs, bytes_accessed=10**6, transcendentals=3 * pairs),
         name="radiate",
-    )(answer, observer, member, info, square)
+    )(answer, observer, distance, member, info, square)
     partial = exchange(partial)
-    summed = jnp.sum(partial, axis=0).reshape(2, 2, obs_distance.shape[0])
-    return summed * obs_distance[None, None, :]
+    return jnp.sum(partial, axis=0).reshape(2, 2, obs_distance.shape[0])
 
 
 def solution(mesh):

time: 97.9 us -> 91.5 us (0.935)
  waiting for transfers between devices: 27.2 us -> 18.4 us
  starting transfers between devices: 27.3 us -> 32.9 us
  Pallas kernels: 18.8 us -> 15.5 us
    all_to_all x2, waiting for transfers between devices: 27.2 us -> 16.7 us  [exchange(): lax.all_to_all(value, 'panel', split_axis=0, concat_axis=0, axis_index_gr...]
    ppermute x0 -> x2, starting transfers between devices: none -> 5.41 us  [swap(): lax.ppermute(value, 'panel', [(at, at ^ 1) for at in range(2 * CHIPS)])]
    pallas_call x4, Pallas kernels: 17.8 us -> 14.5 us  [the longest x1 11.4 us: local(): pl.pallas_call(radiate_kernel, out_shape=table, in_specs=[vmem()] * 6, ou...]
    ppermute x0 -> x2, waiting for transfers between devices: none -> 1.72 us  [swap(): lax.ppermute(value, 'panel', [(at, at ^ 1) for at in range(2 * CHIPS)])]
    unnamed x18 -> x16, local copies, waits for them, and re-layouts: 2.21 us -> 1.64 us
  transfers between devices with their start and end apart: 2 -> 4, of which waited for: 2 -> 4; matrix products, arithmetic and copies ran while one was open for 0% -> 0% of each run, Pallas kernels for 1% -> 1%
where the time goes in v3:
time: 91.5 us; the launch traced here: 91.1 us
  starting transfers between devices  32.9 us (36%)
  blocking collectives  21.7 us (24%)
  waiting for transfers between devices  18.4 us (20%)
  Pallas kernels  15.5 us (17%)
  local copies, waits for them, and re-layouts  2.31 us (3%)
    all_to_all x2, starting transfers between devices, exchange(): lax.all_to_all(value, 'panel', split_axis=0, concat_axis=0, axis_index_gr...  27.5 us
    all_to_all x1, blocking collectives, exchange(): lax.all_to_all(value, 'panel', split_axis=0, concat_axis=0, axis_index_gr...  21.7 us
    all_to_all x2, waiting for transfers between devices, exchange(): lax.all_to_all(value, 'panel', split_axis=0, concat_axis=0, axis_index_gr...  16.7 us
    pallas_call x1, Pallas kernels, local(): pl.pallas_call(radiate_kernel, out_shape=table, in_specs=[vmem()] * 6, ou...  11.4 us
    ppermute x2, starting transfers between devices, swap(): lax.ppermute(value, 'panel', [(at, at ^ 1) for at in range(2 * CHIPS)])  5.41 us
  transfers between devices with their start and end apart: 4, of which 4 were waited for; matrix products, arithmetic and copies ran while one was open for 0% of the time, Pallas kernels for 1%

profile of v3, /device:TPU:1, one launch (start us, length us, event | category | flops | bytes accessed | tf_op | source)
XLA Modules:
  0.0 91.1 jit_solution(17649556605483435879)
XLA Ops:
  0.0 1.8 %ask.1.after_ref = f32[64,128]{1,0:T(8,128)} custom-call(s32[1,256]{1,0:T(1,128)} %bitcast.24, s32[1,256]{1,0:T(1,128)} %bitcast.30, f32[1,32]{1,0:T(1,128)} %bitcast.31, f32[1,32]{1,0:T(1,128)} %bitcast.32, f32[1,32]{1,0:T(1,128)} %bitcast.33), custom_call_target="tpu_custom_call" | custom-call | tf_op jit(solution)/shard_map/ask/pallas_call | solution.py:363
  1.8 0.0 copy-start
  1.8 19.3 %all-to-all-start = ((f32[64,1,128]{2,1,0:T(1,128)}), f32[64,1,128]{2,1,0:T(1,128)S(1)}, u32[]{:S(2)}, u32[]{:S(2)}) async-start(f32[64,1,128]{2,1,0:T(1,128)} %bitcast.21), calls=%async_computation | async-start | bytes 65536 | tf_op jit(solution)/shard_map/all_to_all | solution.py:332
  21.1 0.0 copy-start.5
  21.1 0.0 copy-start.6
  21.1 0.0 copy-start.3
  21.2 0.0 copy-start.4
  21.2 0.0 copy-start.2
  21.2 0.0 copy-start.7
  21.2 0.0 copy-done
  21.2 0.6 copy-done.5
  21.8 0.0 copy-done.6
  21.8 0.0 copy-done.3
  21.8 0.0 copy-done.4
  21.8 0.0 copy-done.2
  21.9 0.0 copy-done.7
  21.9 0.0 copy-start.1
  21.9 0.9 %copy-done.1 = f32[4,8,2,1024]{3,2,1,0:T(2,128)S(1)} copy-done((f32[4,8,2,1024]{3,2,1,0:T(2,128)S(1)}, f32[4,8,2,1024]{3,2,1,0:T(2,128)}, u32[]{:S(2)}) %copy-start.1) | copy-done | bytes 262168
  22.8 1.0 %prepare.1 = (f32[16,1024]{1,0:T(8,128)S(1)}, bf16[64,256]{1,0:T(8,128)(2,1)S(1)}, f32[24,256]{1,0:T(8,128)S(1)}, bf16[2,256,128]{2,1,0:T(8,128)(2,1)S(1)}) custom-call(s32[2]{0:T(128)S(1)} %copy-done.7, f32[64,128]{1,0:T(8,128)S(1)} %copy-done, f32[4,8,2,1024]{3,2,1,0:T(2,128)S(1)} %copy-done.1, s32[1,256]{1,0:T(1,128)S(1)} %bitcast.25, ...), custom_call_target="tpu_custom_call" | custom-call | flops 10000000 | bytes 10000000 | tf_op jit(solution)/shard_map/prepare/pallas_call | solution.py:379
  23.8 2.9 %collective-permute-start = (f32[16,1024]{1,0:T(8,128)S(1)}, f32[16,1024]{1,0:T(8,128)S(1)}, u32[]{:S(2)}, u32[]{:S(2)}) collective-permute-start(f32[16,1024]{1,0:T(8,128)S(1)} %get-tuple-element.12.own_ref), channel_id=1, source_target_pairs={{0,4},{4,0},{8,12},{12,8},{16,20},{20,16},{24,28},{28,24},{32,36},... | collective-permute-start | bytes 196616 | tf_op jit(solution)/shard_map/ppermute | solution.py:338
  26.7 0.9 collective-permute-done.mate_ref
  27.6 6.7 %all-to-all-done = f32[64,1,128]{2,1,0:T(1,128)S(1)} async-done(((f32[64,1,128]{2,1,0:T(1,128)}), f32[64,1,128]{2,1,0:T(1,128)S(1)}, u32[]{:S(2)}, u32[]{:S(2)}) %all-to-all-start) | async-done | bytes 32800 | tf_op jit(solution)/shard_map/all_to_all | solution.py:332
  34.2 1.2 %pick.1 = f32[128,128]{1,0:T(8,128)} custom-call(f32[64,128]{1,0:T(8,128)S(1)} %bitcast.18, f32[16,1024]{1,0:T(8,128)S(1)} %get-tuple-element.12.own_ref, f32[16,1024]{1,0:T(8,128)S(1)} %collective-permute-done.mate_ref), custom_call_target="tpu_custom_call" | custom-call | tf_op jit(solution)/shard_map/pick/pallas_call | solution.py:413
  35.4 8.2 %all-to-all-start.1 = ((f32[64,2,128]{2,1,0:T(2,128)}), f32[64,2,128]{2,1,0:T(2,128)S(1)}, u32[]{:S(2)}, u32[]{:S(2)}) async-start(f32[64,2,128]{2,1,0:T(2,128)} %bitcast.12), calls=%async_computation.1 | async-start | bytes 131072 | tf_op jit(solution)/shard_map/all_to_all | solution.py:332
  43.6 2.5 %collective-permute-start.1 = (f32[64,128]{1,0:T(8,128)S(1)}, f32[64,128]{1,0:T(8,128)S(1)}, u32[]{:S(2)}, u32[]{:S(2)}) collective-permute-start(f32[64,128]{1,0:T(8,128)S(1)} %bitcast.19), channel_id=1, source_target_pairs={{0,4},{4,0},{8,12},{12,8},{16,20},{20,16},{24,28},{28,24},{32,36},... | collective-permute-start | bytes 98312 | tf_op jit(solution)/shard_map/ppermute | solution.py:338
  46.1 0.8 collective-permute-done.1.mate_ref
  47.0 0.2 observers.1
  47.1 10.0 %all-to-all-done.1 = f32[64,2,128]{2,1,0:T(2,128)S(1)} async-done(((f32[64,2,128]{2,1,0:T(2,128)}), f32[64,2,128]{2,1,0:T(2,128)S(1)}, u32[]{:S(2)}, u32[]{:S(2)}) %all-to-all-start.1) | async-done | bytes 65568 | tf_op jit(solution)/shard_map/all_to_all | solution.py:332
  57.1 11.4 %radiate.1 = f32[128,128]{1,0:T(8,128)S(1)} custom-call(f32[128,128]{1,0:T(8,128)S(1)} %bitcast.22, bf16[16,128,256]{2,1,0:T(8,128)(2,1)S(1)} %get-tuple-element.14.observer_ref, f32[32,128]{1,0:T(8,128)S(1)} %get-tuple-element.15.distance_ref, bf16[64,256]{1,0:T(8,128)(2,1)S(1)} %get-tuple-element.16.member_ref, f32[24,256]{1,0:T(8,128)S(1)} %get-tuple-element.17.info_ref, ...), custom_call_target="tpu_custom_call" | custom-call | flops 94371840 | bytes 1000000 | tf_op jit(solution)/shard_map/radiate/pallas_call | solution.py:439
  68.5 21.7 %all_to_all.31 = f32[128,1,128]{2,1,0:T(1,128)S(1)} all-to-all(f32[128,1,128]{2,1,0:T(1,128)S(1)} %bitcast.23), channel_id=1, replica_groups=mesh['panel'=128,'obs'=4] {'panel'}, dimensions={0} | all-to-all | bytes 131072 | tf_op jit(solution)/shard_map/all_to_all | solution.py:332
  90.3 0.2 reduce_sum.9
  90.4 0.7 reshape.45
Async XLA Ops:
  1.8 19.4 %copy-start = (f32[64,128]{1,0:T(8,128)S(1)}, f32[64,128]{1,0:T(8,128)}, u32[]{:S(2)}) copy-start(f32[64,128]{1,0:T(8,128)} %ask.1.after_ref) | copy-start | bytes 98308
  1.8 32.4 %all-to-all-start = ((f32[64,1,128]{2,1,0:T(1,128)}), f32[64,1,128]{2,1,0:T(1,128)S(1)}, u32[]{:S(2)}, u32[]{:S(2)}) async-start(f32[64,1,128]{2,1,0:T(1,128)} %bitcast.21), calls=%async_computation | async-start | bytes 65536 | tf_op jit(solution)/shard_map/all_to_all | solution.py:332
  21.1 0.7 copy-start.5
  21.1 0.7 copy-start.6
  21.1 0.7 copy-start.3
  21.2 0.7 copy-start.4
  21.2 0.7 copy-start.2
  21.2 0.7 copy-start.7
  21.9 1.0 %copy-start.1 = (f32[4,8,2,1024]{3,2,1,0:T(2,128)S(1)}, f32[4,8,2,1024]{3,2,1,0:T(2,128)}, u32[]{:S(2)}) copy-start(f32[4,8,2,1024]{3,2,1,0:T(2,128)} %surface_ref.1) | copy-start | bytes 786436
  23.8 3.8 %collective-permute-start = (f32[16,1024]{1,0:T(8,128)S(1)}, f32[16,1024]{1,0:T(8,128)S(1)}, u32[]{:S(2)}, u32[]{:S(2)}) collective-permute-start(f32[16,1024]{1,0:T(8,128)S(1)} %get-tuple-element.12.own_ref), channel_id=1, source_target_pairs={{0,4},{4,0},{8,12},{12,8},{16,20},{20,16},{24,28},{28,24},{32,36},... | collective-permute-start | bytes 196616 | tf_op jit(solution)/shard_map/ppermute | solution.py:338
  35.4 21.8 %all-to-all-start.1 = ((f32[64,2,128]{2,1,0:T(2,128)}), f32[64,2,128]{2,1,0:T(2,128)S(1)}, u32[]{:S(2)}, u32[]{:S(2)}) async-start(f32[64,2,128]{2,1,0:T(2,128)} %bitcast.12), calls=%async_computation.1 | async-start | bytes 131072 | tf_op jit(solution)/shard_map/all_to_all | solution.py:332
  43.6 3.4 %collective-permute-start.1 = (f32[64,128]{1,0:T(8,128)S(1)}, f32[64,128]{1,0:T(8,128)S(1)}, u32[]{:S(2)}, u32[]{:S(2)}) collective-permute-start(f32[64,128]{1,0:T(8,128)S(1)} %bitcast.19), channel_id=1, source_target_pairs={{0,4},{4,0},{8,12},{12,8},{16,20},{20,16},{24,28},{28,24},{32,36},... | collective-permute-start | bytes 98312 | tf_op jit(solution)/shard_map/ppermute | solution.py:338

commit v4 on v3

--- a/solution.py
+++ b/solution.py
@@ -11,6 +11,7 @@
 BASE_WAVE = 2.0
 LANES = 128
 CHIPS = 64
+FIRST = 40
 SLOTS = 16
 MAGIC = 12582912.0
 F32 = jnp.float32
@@ -46,7 +47,7 @@
 
 def chip_mask(owner):
     rows = lax.broadcasted_iota(jnp.int32, (CHIPS, owner.shape[1]), 0)
-    return jnp.where(rows == (owner >> 1), 1.0, 0.0).astype(F32)
+    return jnp.where(rows == ((owner >> 1) + CHIPS - FIRST) % CHIPS, 1.0, 0.0).astype(F32)
 
 
 def slot_of(owner):
@@ -102,7 +103,9 @@
     block = wanted >> 7
     within = wanted & 127
     first = lax.axis_index("panel") % 2 == 0
-    own, mate = own_ref[...], mate_ref[...]
+    own, mate = [
+        jnp.concatenate([ref[at] for at in range(8)], axis=0) for ref in (own_ref, mate_ref)
+    ]
     values = (jnp.where(first, own, mate), jnp.where(first, mate, own))
     chunks = own.shape[1] // LANES
     for slot in range(SLOTS):
@@ -119,18 +122,17 @@
         out_ref[pl.ds(half, CHIPS, stride=2), :] = jnp.transpose(rows_ref[here, :])[0:CHIPS]
 
 
-def prepare_kernel(harmonic_ref, after_ref, surface_ref, *refs, panel_total):
-    values_ref, member_ref, info_ref, panel_ref = refs[5:9]
-    rows_ref, owner_ref, polar_ref, azimuth_ref, radius_ref, area_ref, sem = refs[9:]
-    sources = list(refs[:5])
-    targets = [owner_ref, polar_ref, azimuth_ref, radius_ref, area_ref]
+def select_kernel(harmonic_ref, after_ref, surface_ref, out_ref, sem):
+    sources, targets = [], []
     for var in range(4):
         for which in range(2):
             sources.append(surface_ref.at[var, harmonic_ref[which] - 1])
-            targets.append(rows_ref.at[2 * var + which])
+            targets.append(out_ref.at[2 * var + which])
     fetch(sources, targets, sem)
-    for at in range(8):
-        values_ref[2 * at : 2 * at + 2] = rows_ref[at]
+
+
+def prepare_kernel(harmonic_ref, after_ref, *refs, panel_total):
+    owner_ref, polar_ref, azimuth_ref, radius_ref, area_ref, member_ref, info_ref, panel_ref = refs
     owner = owner_ref[...]
     count = owner.shape[1]
     member_ref[...] = chip_mask(owner).astype(BF16)
@@ -325,10 +327,12 @@
     return pl.BlockSpec(memory_space=pltpu.SMEM)
 
 
-SAME_CORE = [[2 * chip + core for chip in range(CHIPS)] for core in range(2)]
-
-
-def exchange(value, groups=None):
+ORDER = [(FIRST + at) % CHIPS for at in range(CHIPS)]
+SAME_CORE = [[2 * chip + core for chip in ORDER] for core in range(2)]
+ALL_CORES = [[2 * chip + core for chip in ORDER for core in range(2)]]
+
+
+def exchange(value, groups):
     return lax.all_to_all(
         value, "panel", split_axis=0, concat_axis=0, axis_index_groups=groups, tiled=True
     )
@@ -375,39 +379,16 @@
         obs_azimuth.reshape(1, -1),
         obs_distance.reshape(1, -1),
     )
-    cells = surface.shape[3]
-    values, member, info, square = pl.pallas_call(
-        functools.partial(prepare_kernel, panel_total=panel_total),
-        out_shape=(
-            jax.ShapeDtypeStruct((16, cells), F32),
-            jax.ShapeDtypeStruct((CHIPS, per_device), BF16),
-            jax.ShapeDtypeStruct((24, per_device), F32),
-            jax.ShapeDtypeStruct((2, per_device, LANES), BF16),
-        ),
-        in_specs=[smem(), anywhere()] + [hbm()] * 6,
-        out_specs=(vmem(),) * 4,
-        scratch_shapes=[
-            pltpu.VMEM((8, 2, cells), F32),
-            names,
-            line,
-            line,
-            line,
-            line,
-            pltpu.SemaphoreType.DMA((13,)),
-        ],
+    values = pl.pallas_call(
+        select_kernel,
+        out_shape=jax.ShapeDtypeStruct((8, 2, surface.shape[3]), F32),
+        in_specs=[smem(), anywhere(), hbm()],
+        out_specs=vmem(),
+        scratch_shapes=[pltpu.SemaphoreType.DMA((8,))],
         compiler_params=params,
         cost_estimate=pl.CostEstimate(flops=10**7, bytes_accessed=10**7, transcendentals=0),
-        name="prepare",
-    )(
-        harmonic,
-        ask,
-        surface,
-        owner,
-        pan_polar.reshape(1, -1),
-        pan_azimuth.reshape(1, -1),
-        pan_radius.reshape(1, -1),
-        pan_area.reshape(1, -1),
-    )
+        name="select",
+    )(harmonic, ask, surface)
     mate_values = swap(values)
     asked = exchange(ask, SAME_CORE)
     found = pl.pallas_call(
@@ -422,6 +403,27 @@
     answer = exchange(found, SAME_CORE)
     asked, _ = lax.optimization_barrier((asked, found))
     mate_asked = swap(asked)
+    member, info, square = pl.pallas_call(
+        functools.partial(prepare_kernel, panel_total=panel_total),
+        out_shape=(
+            jax.ShapeDtypeStruct((CHIPS, per_device), BF16),
+            jax.ShapeDtypeStruct((24, per_device), F32),
+            jax.ShapeDtypeStruct((2, per_device, LANES), BF16),
+        ),
+        in_specs=[smem(), anywhere()] + [vmem()] * 5,
+        out_specs=(vmem(),) * 3,
+        compiler_params=params,
+        cost_estimate=pl.CostEstimate(flops=10**7, bytes_accessed=10**7, transcendentals=0),
+        name="prepare",
+    )(
+        harmonic,
+        found,
+        owner,
+        pan_polar.reshape(1, -1),
+        pan_azimuth.reshape(1, -1),
+        pan_radius.reshape(1, -1),
+        pan_area.reshape(1, -1),
+    )
     pairs = per_device * 32 * LANES
     observer, distance = pl.pallas_call(
         observers_kernel,
@@ -452,7 +454,7 @@
         cost_estimate=pl.CostEstimate(flops=90 * pairs, bytes_accessed=10**6, transcendentals=3 * pairs),
         name="radiate",
     )(answer, observer, distance, member, info, square)
-    partial = exchange(partial)
+    partial = exchange(partial, ALL_CORES)
     return jnp.sum(partial, axis=0).reshape(2, 2, obs_distance.shape[0])
 
 

time: 91.5 us -> 83.1 us (0.908)
  waiting for transfers between devices: 18.4 us -> 0.89 us
  starting transfers between devices: 32.9 us -> 43.6 us
  blocking collectives: 21.7 us -> 19.6 us
    all_to_all x2, waiting for transfers between devices: 16.7 us -> 0.01 us  [exchange(): lax.all_to_all(value, 'panel', split_axis=0, concat_axis=0, axis_index_gr...]
    all_to_all x2, starting transfers between devices: 27.5 us -> 37.7 us  [exchange(): lax.all_to_all(value, 'panel', split_axis=0, concat_axis=0, axis_index_gr...]
    all_to_all x1, blocking collectives: 21.7 us -> 19.6 us  [exchange(): lax.all_to_all(value, 'panel', split_axis=0, concat_axis=0, axis_index_gr...]
  transfers between devices with their start and end apart: 4 -> 4, of which waited for: 4 -> 1; matrix products, arithmetic and copies ran while one was open for 0% -> 0% of each run, Pallas kernels for 1% -> 2%
where the time goes in v4:
time: 83.1 us; the launch traced here: 82.7 us
  starting transfers between devices  43.6 us (52%)
  blocking collectives  19.6 us (24%)
  Pallas kernels  16 us (19%)
  local copies, waits for them, and re-layouts  2.27 us (3%)
  waiting for transfers between devices  0.89 us (1%)
    all_to_all x2, starting transfers between devices, exchange(): lax.all_to_all(value, 'panel', split_axis=0, concat_axis=0, axis_index_gr...  37.7 us
    all_to_all x1, blocking collectives, exchange(): lax.all_to_all(value, 'panel', split_axis=0, concat_axis=0, axis_index_gr...  19.6 us
    pallas_call x1, Pallas kernels, local(): pl.pallas_call(radiate_kernel, out_shape=table, in_specs=[vmem()] * 6, ou...  11.4 us
    ppermute x2, starting transfers between devices, swap(): lax.ppermute(value, 'panel', [(at, at ^ 1) for at in range(2 * CHIPS)])  5.96 us
    pallas_call x1, Pallas kernels, local(): pl.pallas_call(ask_kernel, out_shape=jax.ShapeDtypeStruct((CHIPS, LANES),...  1.8 us
  transfers between devices with their start and end apart: 4, of which 1 were waited for; matrix products, arithmetic and copies ran while one was open for 0% of the time, Pallas kernels for 2%

profile of v4, /device:TPU:1, one launch (start us, length us, event | category | flops | bytes accessed | tf_op | source)
XLA Modules:
  0.0 82.7 jit_solution(3837206569145531944)
XLA Ops:
  0.0 1.8 %ask.1.after_ref = f32[64,128]{1,0:T(8,128)} custom-call(s32[1,256]{1,0:T(1,128)} %bitcast.24, s32[1,256]{1,0:T(1,128)} %bitcast.30, f32[1,32]{1,0:T(1,128)} %bitcast.31, f32[1,32]{1,0:T(1,128)} %bitcast.32, f32[1,32]{1,0:T(1,128)} %bitcast.33), custom_call_target="tpu_custom_call" | custom-call | tf_op jit(solution)/shard_map/ask/pallas_call | solution.py:367
  1.8 0.0 copy-start
  1.8 0.0 copy-start.3
  1.8 23.1 %all-to-all-start = ((f32[64,1,128]{2,1,0:T(1,128)}), f32[64,1,128]{2,1,0:T(1,128)S(1)}, u32[]{:S(2)}, u32[]{:S(2)}) async-start(f32[64,1,128]{2,1,0:T(1,128)} %bitcast.21), calls=%async_computation | async-start | bytes 65536 | tf_op jit(solution)/shard_map/all_to_all | solution.py:336
  24.9 0.0 copy-done
  24.9 0.0 copy-done.3
  24.9 0.0 copy-start.1
  24.9 0.9 %copy-done.1 = f32[4,8,2,1024]{3,2,1,0:T(2,128)S(1)} copy-done((f32[4,8,2,1024]{3,2,1,0:T(2,128)S(1)}, f32[4,8,2,1024]{3,2,1,0:T(2,128)}, u32[]{:S(2)}) %copy-start.1) | copy-done | bytes 262168
  25.9 0.7 select.1.own_ref
  26.6 3.1 %collective-permute-start = (f32[8,2,1024]{2,1,0:T(2,128)S(1)}, f32[8,2,1024]{2,1,0:T(2,128)S(1)}, u32[]{:S(2)}, u32[]{:S(2)}) collective-permute-start(f32[8,2,1024]{2,1,0:T(2,128)S(1)} %select.1.own_ref), channel_id=1, source_target_pairs={{0,4},{4,0},{8,12},{12,8},{16,20},{20,16},{24,28},{28,24},{32,36},... | collective-permute-start | bytes 196616 | tf_op jit(solution)/shard_map/ppermute | solution.py:342
  29.8 0.9 %collective-permute-done.mate_ref = f32[8,2,1024]{2,1,0:T(2,128)S(1)} collective-permute-done((f32[8,2,1024]{2,1,0:T(2,128)S(1)}, f32[8,2,1024]{2,1,0:T(2,128)S(1)}, u32[]{:S(2)}, u32[]{:S(2)}) %collective-permute-start) | collective-permute-done | bytes 65568 | tf_op jit(solution)/shard_map/ppermute | solution.py:342
  30.6 0.0 all-to-all-done
  30.6 1.2 %pick.1.after_ref = f32[128,128]{1,0:T(8,128)} custom-call(f32[64,128]{1,0:T(8,128)S(1)} %bitcast.18, f32[8,2,1024]{2,1,0:T(2,128)S(1)} %select.1.own_ref, f32[8,2,1024]{2,1,0:T(2,128)S(1)} %collective-permute-done.mate_ref), custom_call_target="tpu_custom_call" | custom-call | tf_op jit(solution)/shard_map/pick/pallas_call | solution.py:394
  31.8 0.0 copy-start.4
  31.8 0.0 copy-start.5
  31.8 0.0 copy-start.6
  31.8 14.6 %all-to-all-start.1 = ((f32[64,2,128]{2,1,0:T(2,128)}), f32[64,2,128]{2,1,0:T(2,128)S(1)}, u32[]{:S(2)}, u32[]{:S(2)}) async-start(f32[64,2,128]{2,1,0:T(2,128)} %bitcast.8), calls=%async_computation.1 | async-start | bytes 131072 | tf_op jit(solution)/shard_map/all_to_all | solution.py:336
  46.4 2.8 %collective-permute-start.1 = (f32[64,128]{1,0:T(8,128)S(1)}, f32[64,128]{1,0:T(8,128)S(1)}, u32[]{:S(2)}, u32[]{:S(2)}) collective-permute-start(f32[64,128]{1,0:T(8,128)S(1)} %bitcast.19), channel_id=1, source_target_pairs={{0,4},{4,0},{8,12},{12,8},{16,20},{20,16},{24,28},{28,24},{32,36},... | collective-permute-start | bytes 98312 | tf_op jit(solution)/shard_map/ppermute | solution.py:342
  49.2 0.0 copy-start.2
  49.3 0.0 copy-done.4
  49.3 0.0 copy-done.5
  49.3 0.0 copy-done.6
  49.3 0.0 copy-done.7
  49.3 0.6 copy-done.2
  49.9 0.7 prepare.1
  50.7 0.0 collective-permute-done.1.mate_ref
  50.7 0.2 observers.1
  50.9 0.0 all-to-all-done.1
  50.9 11.4 %radiate.1 = f32[128,128]{1,0:T(8,128)S(1)} custom-call(f32[128,128]{1,0:T(8,128)S(1)} %bitcast.22, bf16[16,128,256]{2,1,0:T(8,128)(2,1)S(1)} %get-tuple-element.12.observer_ref, f32[32,128]{1,0:T(8,128)S(1)} %get-tuple-element.13.distance_ref, bf16[64,256]{1,0:T(8,128)(2,1)S(1)} %get-tuple-element.14.member_ref, f32[24,256]{1,0:T(8,128)S(1)} %get-tuple-element.15.info_ref, ...), custom_call_target="tpu_custom_call" | custom-call | flops 94371840 | bytes 1000000 | tf_op jit(solution)/shard_map/radiate/pallas_call | solution.py:441
  62.3 19.6 %all_to_all.31 = f32[128,1,128]{2,1,0:T(1,128)S(1)} all-to-all(f32[128,1,128]{2,1,0:T(1,128)S(1)} %bitcast.23), channel_id=1, replica_groups={{320,324,328,332,336,340,344,348,352,356,360,364,368,372,376,380,384,38..., dimensions={0} | all-to-all | bytes 131072 | tf_op jit(solution)/shard_map/all_to_all | solution.py:336
  81.9 0.2 reduce_sum.9
  82.0 0.7 reshape.45
  (1 shorter events, 0.0 us)
Async XLA Ops:
  1.8 23.1 %copy-start = (f32[64,128]{1,0:T(8,128)S(1)}, f32[64,128]{1,0:T(8,128)}, u32[]{:S(2)}) copy-start(f32[64,128]{1,0:T(8,128)} %ask.1.after_ref) | copy-start | bytes 98308
  1.8 23.1 %copy-start.3 = (s32[2]{0:T(128)S(1)}, s32[2]{0:T(128)}, u32[]{:S(2)}) copy-start(s32[2]{0:T(128)} %harmonic_ref.3) | copy-start | bytes 28
  1.8 28.8 %all-to-all-start = ((f32[64,1,128]{2,1,0:T(1,128)}), f32[64,1,128]{2,1,0:T(1,128)S(1)}, u32[]{:S(2)}, u32[]{:S(2)}) async-start(f32[64,1,128]{2,1,0:T(1,128)} %bitcast.21), calls=%async_computation | async-start | bytes 65536 | tf_op jit(solution)/shard_map/all_to_all | solution.py:336
  24.9 1.0 %copy-start.1 = (f32[4,8,2,1024]{3,2,1,0:T(2,128)S(1)}, f32[4,8,2,1024]{3,2,1,0:T(2,128)}, u32[]{:S(2)}) copy-start(f32[4,8,2,1024]{3,2,1,0:T(2,128)} %surface_ref.1) | copy-start | bytes 786436
  26.6 4.0 %collective-permute-start = (f32[8,2,1024]{2,1,0:T(2,128)S(1)}, f32[8,2,1024]{2,1,0:T(2,128)S(1)}, u32[]{:S(2)}, u32[]{:S(2)}) collective-permute-start(f32[8,2,1024]{2,1,0:T(2,128)S(1)} %select.1.own_ref), channel_id=1, source_target_pairs={{0,4},{4,0},{8,12},{12,8},{16,20},{20,16},{24,28},{28,24},{32,36},... | collective-permute-start | bytes 196616 | tf_op jit(solution)/shard_map/ppermute | solution.py:342
  31.8 17.5 %copy-start.4 = (f32[256]{0:T(256)S(1)}, f32[256]{0:T(256)}, u32[]{:S(2)}) copy-start(f32[256]{0:T(256)} %param.14) | copy-start | bytes 3076
  31.8 17.5 %copy-start.5 = (f32[256]{0:T(256)S(1)}, f32[256]{0:T(256)}, u32[]{:S(2)}) copy-start(f32[256]{0:T(256)} %param.15) | copy-start | bytes 3076
  31.8 17.5 %copy-start.6 = (f32[256]{0:T(256)S(1)}, f32[256]{0:T(256)}, u32[]{:S(2)}) copy-start(f32[256]{0:T(256)} %param.16) | copy-start | bytes 3076
  31.8 17.5 %copy-start.7 = (f32[256]{0:T(256)S(1)}, f32[256]{0:T(256)}, u32[]{:S(2)}) copy-start(f32[256]{0:T(256)} %param.17) | copy-start | bytes 3076
  31.8 19.1 %all-to-all-start.1 = ((f32[64,2,128]{2,1,0:T(2,128)}), f32[64,2,128]{2,1,0:T(2,128)S(1)}, u32[]{:S(2)}, u32[]{:S(2)}) async-start(f32[64,2,128]{2,1,0:T(2,128)} %bitcast.8), calls=%async_computation.1 | async-start | bytes 131072 | tf_op jit(solution)/shard_map/all_to_all | solution.py:336
  46.4 4.3 %collective-permute-start.1 = (f32[64,128]{1,0:T(8,128)S(1)}, f32[64,128]{1,0:T(8,128)S(1)}, u32[]{:S(2)}, u32[]{:S(2)}) collective-permute-start(f32[64,128]{1,0:T(8,128)S(1)} %bitcast.19), channel_id=1, source_target_pairs={{0,4},{4,0},{8,12},{12,8},{16,20},{20,16},{24,28},{28,24},{32,36},... | collective-permute-start | bytes 98312 | tf_op jit(solution)/shard_map/ppermute | solution.py:342
  49.2 0.7 copy-start.2

commit v5 on v4

--- a/solution.py
+++ b/solution.py
@@ -158,11 +158,12 @@
     info_ref[8:16] = stack(jnp.zeros_like(radius), -radius, *normal)
     weight = area_ref[...] * (0.25 / (math.pi * math.sqrt(panel_total)))
     waves = [BASE_WAVE * harmonic_ref[which].astype(F32) for which in range(2)]
-    turns = [wave * (1.0 / (2.0 * math.pi)) for wave in waves]
-    info_ref[16:24] = stack(slot_of(owner), weight, *waves, *turns)
+    unit = jnp.full((1, count), waves[0] * (1.0 / (2.0 * math.pi)), F32)
+    weight = weight * (unit * unit * unit)
+    info_ref[16:24] = stack(slot_of(owner), weight, *waves, 1.0 / unit, waves[1] * ((1.0 / (2.0 * math.pi)) / unit))
 
     zero = jnp.zeros((80, count), F32)
-    for at, quantity in enumerate((square, info_ref[8:16])):
+    for at, quantity in enumerate((square * (unit * unit), info_ref[8:16])):
         high, mid, low = split3(quantity)
         tall = jnp.concatenate([high, mid, high, low, mid, high, zero], axis=0)
         for half in range(count // LANES):
@@ -236,7 +237,8 @@
         for quantity in quantities:
             high, mid, low = split3(quantity)
             tall += [high, mid, high, low]
-        push += [wave * press[0], wave * press[1]]
+        scaled = wave * info_ref[20:21]
+        push += [scaled * press[0], scaled * press[1]]
     tall = jnp.concatenate(tall, axis=0)
     low_lanes = lax.broadcasted_iota(jnp.int32, (LANES, LANES), 1) < 32
     push = jnp.concatenate(push + [jnp.zeros((LANES - 4, count), F32)], axis=0)
@@ -252,7 +254,7 @@
     for number in range(2):
         place(4 + number, 0, square_ref[number])
 
-    turns = [jnp.broadcast_to(info_ref[20 + which : 21 + which, 0:LANES], (8, LANES)) for which in range(2)]
+    ratio = jnp.broadcast_to(info_ref[21:22, 0:LANES], (8, LANES))
 
     def project(step, linear_ref):
         views = jnp.concatenate([observer_ref[step * JOIN + at] for at in range(JOIN)], axis=1)
@@ -280,7 +282,7 @@
                 cube = inverse * inverse * inverse
                 twice = cube + cube
                 for which in range(2):
-                    phase = distance * turns[which]
+                    phase = distance * ratio if which else distance
                     phase = phase - jnp.round(phase)
                     z = phase * phase
                     sine = phase * (TAN_TOP[0] + z * TAN_TOP[1])

time: 83.1 us -> 82.9 us (level)
  no operation moved by 1% of the time
where the time goes in v5:
time: 82.9 us; the launch traced here: 82.5 us
  starting transfers between devices  43.6 us (53%)
  blocking collectives  19.6 us (24%)
  Pallas kernels  15.8 us (19%)
  local copies, waits for them, and re-layouts  2.27 us (3%)
  waiting for transfers between devices  0.89 us (1%)
    all_to_all x2, starting transfers between devices, exchange(): lax.all_to_all(value, 'panel', split_axis=0, concat_axis=0, axis_index_gr...  37.7 us
    all_to_all x1, blocking collectives, exchange(): lax.all_to_all(value, 'panel', split_axis=0, concat_axis=0, axis_index_gr...  19.6 us
    pallas_call x1, Pallas kernels, local(): pl.pallas_call(radiate_kernel, out_shape=table, in_specs=[vmem()] * 6, ou...  11.2 us
    ppermute x2, starting transfers between devices, swap(): lax.ppermute(value, 'panel', [(at, at ^ 1) for at in range(2 * CHIPS)])  5.96 us
    pallas_call x1, Pallas kernels, local(): pl.pallas_call(ask_kernel, out_shape=jax.ShapeDtypeStruct((CHIPS, LANES),...  1.8 us
  transfers between devices with their start and end apart: 4, of which 1 were waited for; matrix products, arithmetic and copies ran while one was open for 0% of the time, Pallas kernels for 2%

profile of v5, /device:TPU:1, one launch (start us, length us, event | category | flops | bytes accessed | tf_op | source)
XLA Modules:
  0.0 82.5 jit_solution(16930364483907566528)
XLA Ops:
  0.0 1.8 %ask.1.after_ref = f32[64,128]{1,0:T(8,128)} custom-call(s32[1,256]{1,0:T(1,128)} %bitcast.24, s32[1,256]{1,0:T(1,128)} %bitcast.30, f32[1,32]{1,0:T(1,128)} %bitcast.31, f32[1,32]{1,0:T(1,128)} %bitcast.32, f32[1,32]{1,0:T(1,128)} %bitcast.33), custom_call_target="tpu_custom_call" | custom-call | tf_op jit(solution)/shard_map/ask/pallas_call | solution.py:369
  1.8 0.0 copy-start
  1.8 0.0 copy-start.3
  1.8 23.1 %all-to-all-start = ((f32[64,1,128]{2,1,0:T(1,128)}), f32[64,1,128]{2,1,0:T(1,128)S(1)}, u32[]{:S(2)}, u32[]{:S(2)}) async-start(f32[64,1,128]{2,1,0:T(1,128)} %bitcast.21), calls=%async_computation | async-start | bytes 65536 | tf_op jit(solution)/shard_map/all_to_all | solution.py:338
  24.9 0.0 copy-done
  24.9 0.0 copy-done.3
  24.9 0.0 copy-start.1
  24.9 0.9 %copy-done.1 = f32[4,8,2,1024]{3,2,1,0:T(2,128)S(1)} copy-done((f32[4,8,2,1024]{3,2,1,0:T(2,128)S(1)}, f32[4,8,2,1024]{3,2,1,0:T(2,128)}, u32[]{:S(2)}) %copy-start.1) | copy-done | bytes 262168
  25.9 0.7 select.1.own_ref
  26.6 3.1 %collective-permute-start = (f32[8,2,1024]{2,1,0:T(2,128)S(1)}, f32[8,2,1024]{2,1,0:T(2,128)S(1)}, u32[]{:S(2)}, u32[]{:S(2)}) collective-permute-start(f32[8,2,1024]{2,1,0:T(2,128)S(1)} %select.1.own_ref), channel_id=1, source_target_pairs={{0,4},{4,0},{8,12},{12,8},{16,20},{20,16},{24,28},{28,24},{32,36},... | collective-permute-start | bytes 196616 | tf_op jit(solution)/shard_map/ppermute | solution.py:344
  29.8 0.9 %collective-permute-done.mate_ref = f32[8,2,1024]{2,1,0:T(2,128)S(1)} collective-permute-done((f32[8,2,1024]{2,1,0:T(2,128)S(1)}, f32[8,2,1024]{2,1,0:T(2,128)S(1)}, u32[]{:S(2)}, u32[]{:S(2)}) %collective-permute-start) | collective-permute-done | bytes 65568 | tf_op jit(solution)/shard_map/ppermute | solution.py:344
  30.6 0.0 all-to-all-done
  30.6 1.2 %pick.1.after_ref = f32[128,128]{1,0:T(8,128)} custom-call(f32[64,128]{1,0:T(8,128)S(1)} %bitcast.18, f32[8,2,1024]{2,1,0:T(2,128)S(1)} %select.1.own_ref, f32[8,2,1024]{2,1,0:T(2,128)S(1)} %collective-permute-done.mate_ref), custom_call_target="tpu_custom_call" | custom-call | tf_op jit(solution)/shard_map/pick/pallas_call | solution.py:396
  31.8 0.0 copy-start.4
  31.8 0.0 copy-start.5
  31.8 0.0 copy-start.6
  31.8 14.6 %all-to-all-start.1 = ((f32[64,2,128]{2,1,0:T(2,128)}), f32[64,2,128]{2,1,0:T(2,128)S(1)}, u32[]{:S(2)}, u32[]{:S(2)}) async-start(f32[64,2,128]{2,1,0:T(2,128)} %bitcast.8), calls=%async_computation.1 | async-start | bytes 131072 | tf_op jit(solution)/shard_map/all_to_all | solution.py:338
  46.4 2.8 %collective-permute-start.1 = (f32[64,128]{1,0:T(8,128)S(1)}, f32[64,128]{1,0:T(8,128)S(1)}, u32[]{:S(2)}, u32[]{:S(2)}) collective-permute-start(f32[64,128]{1,0:T(8,128)S(1)} %bitcast.19), channel_id=1, source_target_pairs={{0,4},{4,0},{8,12},{12,8},{16,20},{20,16},{24,28},{28,24},{32,36},... | collective-permute-start | bytes 98312 | tf_op jit(solution)/shard_map/ppermute | solution.py:344
  49.2 0.0 copy-start.2
  49.3 0.0 copy-done.4
  49.3 0.0 copy-done.5
  49.3 0.0 copy-done.6
  49.3 0.0 copy-done.7
  49.3 0.6 copy-done.2
  49.9 0.7 prepare.1
  50.7 0.0 collective-permute-done.1.mate_ref
  50.7 0.2 observers.1
  50.9 0.0 all-to-all-done.1
  50.9 11.2 %radiate.1 = f32[128,128]{1,0:T(8,128)S(1)} custom-call(f32[128,128]{1,0:T(8,128)S(1)} %bitcast.22, bf16[16,128,256]{2,1,0:T(8,128)(2,1)S(1)} %get-tuple-element.12.observer_ref, f32[32,128]{1,0:T(8,128)S(1)} %get-tuple-element.13.distance_ref, bf16[64,256]{1,0:T(8,128)(2,1)S(1)} %get-tuple-element.14.member_ref, f32[24,256]{1,0:T(8,128)S(1)} %get-tuple-element.15.info_ref, ...), custom_call_target="tpu_custom_call" | custom-call | flops 94371840 | bytes 1000000 | tf_op jit(solution)/shard_map/radiate/pallas_call | solution.py:443
  62.1 19.6 %all_to_all.31 = f32[128,1,128]{2,1,0:T(1,128)S(1)} all-to-all(f32[128,1,128]{2,1,0:T(1,128)S(1)} %bitcast.23), channel_id=1, replica_groups={{320,324,328,332,336,340,344,348,352,356,360,364,368,372,376,380,384,38..., dimensions={0} | all-to-all | bytes 131072 | tf_op jit(solution)/shard_map/all_to_all | solution.py:338
  81.7 0.2 reduce_sum.9
  81.8 0.7 reshape.45
  (1 shorter events, 0.0 us)
Async XLA Ops:
  1.8 23.1 %copy-start = (f32[64,128]{1,0:T(8,128)S(1)}, f32[64,128]{1,0:T(8,128)}, u32[]{:S(2)}) copy-start(f32[64,128]{1,0:T(8,128)} %ask.1.after_ref) | copy-start | bytes 98308
  1.8 23.1 %copy-start.3 = (s32[2]{0:T(128)S(1)}, s32[2]{0:T(128)}, u32[]{:S(2)}) copy-start(s32[2]{0:T(128)} %harmonic_ref.3) | copy-start | bytes 28
  1.8 28.8 %all-to-all-start = ((f32[64,1,128]{2,1,0:T(1,128)}), f32[64,1,128]{2,1,0:T(1,128)S(1)}, u32[]{:S(2)}, u32[]{:S(2)}) async-start(f32[64,1,128]{2,1,0:T(1,128)} %bitcast.21), calls=%async_computation | async-start | bytes 65536 | tf_op jit(solution)/shard_map/all_to_all | solution.py:338
  24.9 1.0 %copy-start.1 = (f32[4,8,2,1024]{3,2,1,0:T(2,128)S(1)}, f32[4,8,2,1024]{3,2,1,0:T(2,128)}, u32[]{:S(2)}) copy-start(f32[4,8,2,1024]{3,2,1,0:T(2,128)} %surface_ref.1) | copy-start | bytes 786436
  26.6 4.0 %collective-permute-start = (f32[8,2,1024]{2,1,0:T(2,128)S(1)}, f32[8,2,1024]{2,1,0:T(2,128)S(1)}, u32[]{:S(2)}, u32[]{:S(2)}) collective-permute-start(f32[8,2,1024]{2,1,0:T(2,128)S(1)} %select.1.own_ref), channel_id=1, source_target_pairs={{0,4},{4,0},{8,12},{12,8},{16,20},{20,16},{24,28},{28,24},{32,36},... | collective-permute-start | bytes 196616 | tf_op jit(solution)/shard_map/ppermute | solution.py:344
  31.8 17.5 %copy-start.4 = (f32[256]{0:T(256)S(1)}, f32[256]{0:T(256)}, u32[]{:S(2)}) copy-start(f32[256]{0:T(256)} %param.14) | copy-start | bytes 3076
  31.8 17.5 %copy-start.5 = (f32[256]{0:T(256)S(1)}, f32[256]{0:T(256)}, u32[]{:S(2)}) copy-start(f32[256]{0:T(256)} %param.15) | copy-start | bytes 3076
  31.8 17.5 %copy-start.6 = (f32[256]{0:T(256)S(1)}, f32[256]{0:T(256)}, u32[]{:S(2)}) copy-start(f32[256]{0:T(256)} %param.16) | copy-start | bytes 3076
  31.8 17.5 %copy-start.7 = (f32[256]{0:T(256)S(1)}, f32[256]{0:T(256)}, u32[]{:S(2)}) copy-start(f32[256]{0:T(256)} %param.17) | copy-start | bytes 3076
  31.8 19.1 %all-to-all-start.1 = ((f32[64,2,128]{2,1,0:T(2,128)}), f32[64,2,128]{2,1,0:T(2,128)S(1)}, u32[]{:S(2)}, u32[]{:S(2)}) async-start(f32[64,2,128]{2,1,0:T(2,128)} %bitcast.8), calls=%async_computation.1 | async-start | bytes 131072 | tf_op jit(solution)/shard_map/all_to_all | solution.py:338
  46.4 4.3 %collective-permute-start.1 = (f32[64,128]{1,0:T(8,128)S(1)}, f32[64,128]{1,0:T(8,128)S(1)}, u32[]{:S(2)}, u32[]{:S(2)}) collective-permute-start(f32[64,128]{1,0:T(8,128)S(1)} %bitcast.19), channel_id=1, source_target_pairs={{0,4},{4,0},{8,12},{12,8},{16,20},{20,16},{24,28},{28,24},{32,36},... | collective-permute-start | bytes 98312 | tf_op jit(solution)/shard_map/ppermute | solution.py:344
  49.2 0.7 copy-start.2

commit v6 on v5

--- a/solution.py
+++ b/solution.py
@@ -311,6 +311,15 @@
         total = total + sums_ref[pl.ds(at, LANES, stride=8), :]
     total = total * jnp.concatenate([distance_ref[...]] * 4, axis=0)
     out_ref[...] = jnp.transpose(total)
+
+
+def finish_kernel(part_ref, out_ref):
+    line = jnp.sum(part_ref[...], axis=0, keepdims=True)
+    width = out_ref.shape[2]
+    for which in range(2):
+        for part in range(2):
+            at = (2 * which + part) * width
+            out_ref[which, part : part + 1, :] = line[:, at : at + width]
 
 
 def vmem():
@@ -457,7 +466,14 @@
         name="radiate",
     )(answer, observer, distance, member, info, square)
     partial = exchange(partial, ALL_CORES)
-    return jnp.sum(partial, axis=0).reshape(2, 2, obs_distance.shape[0])
+    return pl.pallas_call(
+        finish_kernel,
+        out_shape=jax.ShapeDtypeStruct((2, 2, obs_distance.shape[0]), F32),
+        in_specs=[vmem()],
+        out_specs=vmem(),
+        compiler_params=params,
+        name="finish",
+    )(partial)
 
 
 def solution(mesh):

time: 82.9 us -> 82.8 us (level)
  no operation moved by 1% of the time
where the time goes in v6:
time: 82.8 us; the launch traced here: 82.4 us
  starting transfers between devices  43.6 us (53%)
  blocking collectives  19.6 us (24%)
  Pallas kernels  16.4 us (20%)
  local copies, waits for them, and re-layouts  1.6 us (2%)
  waiting for transfers between devices  0.89 us (1%)
    all_to_all x2, starting transfers between devices, exchange(): lax.all_to_all(value, 'panel', split_axis=0, concat_axis=0, axis_index_gr...  37.7 us
    all_to_all x1, blocking collectives, exchange(): lax.all_to_all(value, 'panel', split_axis=0, concat_axis=0, axis_index_gr...  19.6 us
    pallas_call x1, Pallas kernels, local(): pl.pallas_call(radiate_kernel, out_shape=table, in_specs=[vmem()] * 6, ou...  11.2 us
    ppermute x2, starting transfers between devices, swap(): lax.ppermute(value, 'panel', [(at, at ^ 1) for at in range(2 * CHIPS)])  5.96 us
    pallas_call x1, Pallas kernels, local(): pl.pallas_call(ask_kernel, out_shape=jax.ShapeDtypeStruct((CHIPS, LANES),...  1.79 us
  transfers between devices with their start and end apart: 4, of which 1 were waited for; matrix products, arithmetic and copies ran while one was open for 0% of the time, Pallas kernels for 2%

profile of v6, /device:TPU:1, one launch (start us, length us, event | category | flops | bytes accessed | tf_op | source)
XLA Modules:
  0.0 82.4 jit_solution(13187205467500635422)
XLA Ops:
  0.0 1.8 %ask.1.after_ref = f32[64,128]{1,0:T(8,128)} custom-call(s32[1,256]{1,0:T(1,128)} %bitcast.26, s32[1,256]{1,0:T(1,128)} %bitcast.32, f32[1,32]{1,0:T(1,128)} %bitcast.33, f32[1,32]{1,0:T(1,128)} %bitcast.34, f32[1,32]{1,0:T(1,128)} %bitcast.35), custom_call_target="tpu_custom_call" | custom-call | tf_op jit(solution)/shard_map/ask/pallas_call | solution.py:378
  1.8 0.0 copy-start
  1.8 0.0 copy-start.3
  1.8 23.1 %all-to-all-start = ((f32[64,1,128]{2,1,0:T(1,128)}), f32[64,1,128]{2,1,0:T(1,128)S(1)}, u32[]{:S(2)}, u32[]{:S(2)}) async-start(f32[64,1,128]{2,1,0:T(1,128)} %bitcast.22), calls=%async_computation | async-start | bytes 65536 | tf_op jit(solution)/shard_map/all_to_all | solution.py:347
  24.9 0.0 copy-done
  24.9 0.0 copy-done.3
  24.9 0.0 copy-start.1
  24.9 0.9 %copy-done.1 = f32[4,8,2,1024]{3,2,1,0:T(2,128)S(1)} copy-done((f32[4,8,2,1024]{3,2,1,0:T(2,128)S(1)}, f32[4,8,2,1024]{3,2,1,0:T(2,128)}, u32[]{:S(2)}) %copy-start.1) | copy-done | bytes 262168
  25.9 0.7 select.1.own_ref
  26.6 3.1 %collective-permute-start = (f32[8,2,1024]{2,1,0:T(2,128)S(1)}, f32[8,2,1024]{2,1,0:T(2,128)S(1)}, u32[]{:S(2)}, u32[]{:S(2)}) collective-permute-start(f32[8,2,1024]{2,1,0:T(2,128)S(1)} %select.1.own_ref), channel_id=1, source_target_pairs={{0,4},{4,0},{8,12},{12,8},{16,20},{20,16},{24,28},{28,24},{32,36},... | collective-permute-start | bytes 196616 | tf_op jit(solution)/shard_map/ppermute | solution.py:353
  29.7 0.9 %collective-permute-done.mate_ref = f32[8,2,1024]{2,1,0:T(2,128)S(1)} collective-permute-done((f32[8,2,1024]{2,1,0:T(2,128)S(1)}, f32[8,2,1024]{2,1,0:T(2,128)S(1)}, u32[]{:S(2)}, u32[]{:S(2)}) %collective-permute-start) | collective-permute-done | bytes 65568 | tf_op jit(solution)/shard_map/ppermute | solution.py:353
  30.6 0.0 all-to-all-done
  30.6 1.1 %pick.1.after_ref = f32[128,128]{1,0:T(8,128)} custom-call(f32[64,128]{1,0:T(8,128)S(1)} %bitcast.19, f32[8,2,1024]{2,1,0:T(2,128)S(1)} %select.1.own_ref, f32[8,2,1024]{2,1,0:T(2,128)S(1)} %collective-permute-done.mate_ref), custom_call_target="tpu_custom_call" | custom-call | tf_op jit(solution)/shard_map/pick/pallas_call | solution.py:405
  31.8 0.0 copy-start.4
  31.8 0.0 copy-start.5
  31.8 0.0 copy-start.6
  31.8 0.0 copy-start.7
  31.8 14.6 %all-to-all-start.1 = ((f32[64,2,128]{2,1,0:T(2,128)}), f32[64,2,128]{2,1,0:T(2,128)S(1)}, u32[]{:S(2)}, u32[]{:S(2)}) async-start(f32[64,2,128]{2,1,0:T(2,128)} %bitcast.8), calls=%async_computation.1 | async-start | bytes 131072 | tf_op jit(solution)/shard_map/all_to_all | solution.py:347
  46.4 2.8 %collective-permute-start.1 = (f32[64,128]{1,0:T(8,128)S(1)}, f32[64,128]{1,0:T(8,128)S(1)}, u32[]{:S(2)}, u32[]{:S(2)}) collective-permute-start(f32[64,128]{1,0:T(8,128)S(1)} %bitcast.20), channel_id=1, source_target_pairs={{0,4},{4,0},{8,12},{12,8},{16,20},{20,16},{24,28},{28,24},{32,36},... | collective-permute-start | bytes 98312 | tf_op jit(solution)/shard_map/ppermute | solution.py:353
  49.2 0.0 copy-start.2
  49.2 0.0 copy-done.4
  49.2 0.0 copy-done.5
  49.3 0.0 copy-done.6
  49.3 0.0 copy-done.7
  49.3 0.6 copy-done.2
  49.9 0.7 prepare.1
  50.6 0.0 collective-permute-done.1.mate_ref
  50.7 0.2 observers.1
  50.9 0.0 all-to-all-done.1
  50.9 11.2 %radiate.1 = f32[128,128]{1,0:T(8,128)S(1)} custom-call(f32[128,128]{1,0:T(8,128)S(1)} %bitcast.24, bf16[16,128,256]{2,1,0:T(8,128)(2,1)S(1)} %get-tuple-element.12.observer_ref, f32[32,128]{1,0:T(8,128)S(1)} %get-tuple-element.13.distance_ref, bf16[64,256]{1,0:T(8,128)(2,1)S(1)} %get-tuple-element.14.member_ref, f32[24,256]{1,0:T(8,128)S(1)} %get-tuple-element.15.info_ref, ...), custom_call_target="tpu_custom_call" | custom-call | flops 94371840 | bytes 1000000 | tf_op jit(solution)/shard_map/radiate/pallas_call | solution.py:452
  62.1 19.6 %all_to_all.33 = f32[128,1,128]{2,1,0:T(1,128)S(1)} all-to-all(f32[128,1,128]{2,1,0:T(1,128)S(1)} %bitcast.25), channel_id=1, replica_groups={{320,324,328,332,336,340,344,348,352,356,360,364,368,372,376,380,384,38..., dimensions={0} | all-to-all | bytes 131072 | tf_op jit(solution)/shard_map/all_to_all | solution.py:347
  81.7 0.7 finish.1
Async XLA Ops:
  1.8 23.1 %copy-start = (f32[64,128]{1,0:T(8,128)S(1)}, f32[64,128]{1,0:T(8,128)}, u32[]{:S(2)}) copy-start(f32[64,128]{1,0:T(8,128)} %ask.1.after_ref) | copy-start | bytes 98308
  1.8 23.1 %copy-start.3 = (s32[2]{0:T(128)S(1)}, s32[2]{0:T(128)}, u32[]{:S(2)}) copy-start(s32[2]{0:T(128)} %harmonic_ref.3) | copy-start | bytes 28
  1.8 28.8 %all-to-all-start = ((f32[64,1,128]{2,1,0:T(1,128)}), f32[64,1,128]{2,1,0:T(1,128)S(1)}, u32[]{:S(2)}, u32[]{:S(2)}) async-start(f32[64,1,128]{2,1,0:T(1,128)} %bitcast.22), calls=%async_computation | async-start | bytes 65536 | tf_op jit(solution)/shard_map/all_to_all | solution.py:347
  24.9 1.0 %copy-start.1 = (f32[4,8,2,1024]{3,2,1,0:T(2,128)S(1)}, f32[4,8,2,1024]{3,2,1,0:T(2,128)}, u32[]{:S(2)}) copy-start(f32[4,8,2,1024]{3,2,1,0:T(2,128)} %surface_ref.1) | copy-start | bytes 786436
  26.6 4.0 %collective-permute-start = (f32[8,2,1024]{2,1,0:T(2,128)S(1)}, f32[8,2,1024]{2,1,0:T(2,128)S(1)}, u32[]{:S(2)}, u32[]{:S(2)}) collective-permute-start(f32[8,2,1024]{2,1,0:T(2,128)S(1)} %select.1.own_ref), channel_id=1, source_target_pairs={{0,4},{4,0},{8,12},{12,8},{16,20},{20,16},{24,28},{28,24},{32,36},... | collective-permute-start | bytes 196616 | tf_op jit(solution)/shard_map/ppermute | solution.py:353
  31.8 17.5 %copy-start.4 = (f32[256]{0:T(256)S(1)}, f32[256]{0:T(256)}, u32[]{:S(2)}) copy-start(f32[256]{0:T(256)} %param.14) | copy-start | bytes 3076
  31.8 17.5 %copy-start.5 = (f32[256]{0:T(256)S(1)}, f32[256]{0:T(256)}, u32[]{:S(2)}) copy-start(f32[256]{0:T(256)} %param.15) | copy-start | bytes 3076
  31.8 17.5 %copy-start.6 = (f32[256]{0:T(256)S(1)}, f32[256]{0:T(256)}, u32[]{:S(2)}) copy-start(f32[256]{0:T(256)} %param.16) | copy-start | bytes 3076
  31.8 17.5 %copy-start.7 = (f32[256]{0:T(256)S(1)}, f32[256]{0:T(256)}, u32[]{:S(2)}) copy-start(f32[256]{0:T(256)} %param.17) | copy-start | bytes 3076
  31.8 19.1 %all-to-all-start.1 = ((f32[64,2,128]{2,1,0:T(2,128)}), f32[64,2,128]{2,1,0:T(2,128)S(1)}, u32[]{:S(2)}, u32[]{:S(2)}) async-start(f32[64,2,128]{2,1,0:T(2,128)} %bitcast.8), calls=%async_computation.1 | async-start | bytes 131072 | tf_op jit(solution)/shard_map/all_to_all | solution.py:347
  46.4 4.3 %collective-permute-start.1 = (f32[64,128]{1,0:T(8,128)S(1)}, f32[64,128]{1,0:T(8,128)S(1)}, u32[]{:S(2)}, u32[]{:S(2)}) collective-permute-start(f32[64,128]{1,0:T(8,128)S(1)} %bitcast.20), channel_id=1, source_target_pairs={{0,4},{4,0},{8,12},{12,8},{16,20},{20,16},{24,28},{28,24},{32,36},... | collective-permute-start | bytes 98312 | tf_op jit(solution)/shard_map/ppermute | solution.py:353
  49.2 0.7 copy-start.2
